TPU v7x, 256 devices: a whole 4x4x8 slice. The times are simulated.
256 devices in a mesh: frame: 32 (over x, z), rec: 8 (over y, core).
Axes of the slice: x: 4, y: 4, z: 8, core: 2. Of those that a mesh axis runs over, the one named last changes fastest.
Arguments:
- inputs: bfloat16 [8, 32768, 512], P('rec', 'frame'), may hold values from -6 to 6
- conv_weight: bfloat16 [5, 512, 512], replicated, may hold values from -4 to 4
- conv_bias: float32 [512], replicated, may hold values from -3 to 3
- labels: int32 [8, 32768, 512], P('rec', 'frame'), may hold values 0 or 1
- rec_span: int32 [2, 8, 32768], P(None, 'rec', 'frame'), may hold values from 0 to 1023, as said below
Outputs:
- features: bfloat16 [8, 32768, 512], P('rec', 'frame')
- probe_weights: float32 [512, 512], replicated
Inputs may be any that keep to these rules, and one draw needn't show every extreme that they name: Each stream is a series of whole recordings of at most 1024 frames, the last one possibly cut by the stream's end: rec_span[0, g, t] counts the frames of t's recording before t and rec_span[1, g, t] those after t within the stream; in every stream some recording has exactly 1024 frames.
All inputs are finite; a program needn't handle non-finite values. No bound on the sum of `labels` on one device may be relied on, other than what follows from the above.
Results may differ from a plain program's by a relative error of at most 0.0035.
The roundings to bfloat16 on the way count: a program that leaves them out, or rounds other values in their place, can miss the bound.
Values may be sent and summed in bfloat16 or wider, within the bound.
No kernel may reach another device: no remote copies, remote signals or barrier semaphores. Data moves between devices by JAX's collectives and lax.ppermute only.
A program may use at most 64 MiB of HBM per device.

v0:
```python
import functools
import math

import jax
import jax.numpy as jnp
from jax import lax
from jax.experimental import pallas as pl
from jax.experimental.pallas import tpu as pltpu
from jax.sharding import Mesh, PartitionSpec as P

RIDGE = 0.1
BLOCK = 128
GROUP = 8


def frame_halo(rows, width):
    size = lax.axis_size(("x", "z"))
    up = [(i, i + 1) for i in range(size - 1)]
    down = [(j, i) for i, j in up]
    before = lax.ppermute(rows[-width:], ("x", "z"), up)
    after = lax.ppermute(rows[:width], ("x", "z"), down)
    return before, after


def all_sum(halves):
    core = lax.axis_index("core")
    swap = [(0, 1), (1, 0)]
    keep = jnp.where(core == 0, halves[0], halves[1])
    send = jnp.where(core == 0, halves[1], halves[0])
    part = keep + lax.ppermute(send, "core", swap)
    peers = lax.axis_size(("x", "y"))
    rows = part.shape[0] // peers
    chunks = lax.all_to_all(
        part.reshape(peers, rows, BLOCK), ("x", "y"), split_axis=0, concat_axis=0, tiled=True
    )
    chunk = jnp.sum(chunks, axis=0)
    for bit in (1, 2, 4):
        chunk = chunk + lax.ppermute(
            chunk, "z", [(i, i ^ bit) for i in range(lax.axis_size("z"))]
        )
    spread = jnp.broadcast_to(chunk[None], (peers, rows, BLOCK))
    full = lax.all_to_all(spread, ("x", "y"), split_axis=0, concat_axis=0, tiled=True)
    mine = full.reshape(peers * rows, BLOCK)
    other = lax.ppermute(mine, "core", swap)
    return mine, other


def group_inverse(diag, rows):
    size = len(rows)
    for j in range(0, size, 2):
        a, b, c = diag[j][j], diag[j][j + 1], diag[j + 1][j + 1]
        scale = 1.0 / (a * c - b * b)
        left = [diag[i][j] for i in range(size)]
        right = [diag[i][j + 1] for i in range(size)]

        def solved(upper, lower):
            return (c * upper - b * lower) * scale, (a * lower - b * upper) * scale

        new = {k: solved(diag[j][k], diag[j + 1][k]) for k in range(j + 2, size)}
        for i in range(size):
            if i in (j, j + 1):
                continue
            for k in range(max(j + 2, i) if i > j else j + 2, size):
                diag[i][k] = diag[i][k] - left[i] * new[k][0] - right[i] * new[k][1]
                if i > j:
                    diag[k][i] = diag[i][k]
        for k in range(j + 2, size):
            diag[j][k], diag[j + 1][k] = new[k]
        rows[j], rows[j + 1] = solved(rows[j], rows[j + 1])
        for i in range(size):
            if i not in (j, j + 1):
                rows[i] = rows[i] - left[i] * rows[j] - right[i] * rows[j + 1]
    return rows


def spd_inverse(block):
    groups = BLOCK // GROUP
    tile = (GROUP, BLOCK)
    lane = lax.broadcasted_iota(jnp.int32, tile, 1)
    sublane = lax.broadcasted_iota(jnp.int32, tile, 0)
    part = [block[h * GROUP : (h + 1) * GROUP] for h in range(groups)]

    def spread(value):
        return jnp.broadcast_to(value, tile)

    def columns(h, first):
        return [spread(part[h][:, first + j : first + j + 1]) for j in range(GROUP)]

    def pivots(g):
        first = g * GROUP
        inside = (lane >= first) & (lane < first + GROUP)
        cols = columns(g, first)
        diag = [[None] * GROUP for _ in range(GROUP)]
        for i in range(GROUP):
            for j in range(i, GROUP):
                diag[i][j] = diag[j][i] = spread(cols[i][j : j + 1])
        rows = [
            jnp.where(
                lane == first + i, 1.0, jnp.where(inside, 0.0, spread(part[g][i : i + 1]))
            )
            for i in range(GROUP)
        ]
        return inside, diag, rows

    ahead = pivots(0)
    for g in range(groups):
        inside, diag, rows = ahead
        others = [(g + n) % groups for n in range(1, groups)]
        cols = {h: columns(h, g * GROUP) for h in others}
        rows = group_inverse(diag, rows)

        def eliminate(h):
            terms = [cols[h][j] * rows[j] for j in range(GROUP)]
            while len(terms) > 1:
                terms = [terms[n] + terms[n + 1] for n in range(0, len(terms), 2)]
            part[h] = jnp.where(inside, 0.0, part[h]) - terms[0]

        eliminate(others[0])
        if g + 1 < groups:
            ahead = pivots(g + 1)
        for h in others[1:]:
            eliminate(h)
        for i in range(GROUP):
            part[g] = jnp.where(sublane == i, rows[i], part[g])
    return jnp.concatenate(part, axis=0)


def dot32(a, b):
    return jnp.dot(a, b, precision=lax.Precision.HIGHEST, preferred_element_type=jnp.float32)


def solve_kernel(kept, row_blocks, col_blocks, frame_count, core_ref, mine_ref, other_ref, out_ref, work):
    core = core_ref[0]
    half = mine_ref.shape[0] // BLOCK

    def summed(n):
        owner, place = divmod(n, half)
        at = pl.ds(place * BLOCK, BLOCK)
        return jnp.where(core == owner, mine_ref[at, :], other_ref[at, :])

    def span(i, j=None):
        return slice(i * BLOCK, (i + 1 if j is None else j) * BLOCK)

    totals = summed(len(kept))[:col_blocks]
    diagonal = lax.broadcasted_iota(jnp.int32, (BLOCK, BLOCK), 0) == lax.broadcasted_iota(
        jnp.int32, (BLOCK, BLOCK), 1
    )
    across = [jnp.broadcast_to(totals[j : j + 1], (BLOCK, BLOCK)) for j in range(col_blocks)]
    down = [across[i].T for i in range(row_blocks)]
    for n, (i, j) in enumerate(kept):
        centred = summed(n) - down[i] * across[j] / frame_count
        if j >= row_blocks:
            work[span(i), span(j)] = centred / math.sqrt(frame_count)
        else:
            block = centred / frame_count
            work[span(i), span(j)] = jnp.where(diagonal, block + RIDGE, block) if i == j else block

    for k in range(row_blocks):
        rest = span(k + 1, col_blocks)
        inverse = spd_inverse(work[span(k), span(k)])
        flipped = {i: work[span(k), span(i)].T for i in range(k + 1, row_blocks)}
        solved = dot32(inverse, work[span(k), rest])
        work[span(k), rest] = solved
        for i in range(k + 1, row_blocks):
            at = span(i, col_blocks)
            work[span(i), at] -= dot32(flipped[i], solved[:, (i - k - 1) * BLOCK :])
        if k:
            work[span(0, k), rest] -= dot32(work[span(0, k), span(k)], solved)
    out_ref[...] = work[:, span(row_blocks, col_blocks)]


def ridge_solve(mine, other, kept, row_blocks, col_blocks, frame_count):
    core = lax.axis_index("core").astype(jnp.int32)[None]
    return pl.pallas_call(
        functools.partial(solve_kernel, kept, row_blocks, col_blocks, float(frame_count)),
        out_shape=jax.ShapeDtypeStruct(
            (row_blocks * BLOCK, (col_blocks - row_blocks) * BLOCK), jnp.float32
        ),
        in_specs=[
            pl.BlockSpec(memory_space=pltpu.SMEM),
            pl.BlockSpec(memory_space=pltpu.VMEM),
            pl.BlockSpec(memory_space=pltpu.VMEM),
        ],
        out_specs=pl.BlockSpec(memory_space=pltpu.VMEM),
        scratch_shapes=[pltpu.VMEM((row_blocks * BLOCK, col_blocks * BLOCK), jnp.float32)],
        compiler_params=pltpu.CompilerParams(vmem_limit_bytes=40 * 1024 * 1024),
        name="ridge_solve",
    )(core, mine, other)


def per_device(inputs, conv_weight, conv_bias, labels, rec_span):
    tap_count = conv_weight.shape[0]
    half_width = tap_count // 2
    shard_rows = inputs.shape[1]
    feat_width = conv_weight.shape[2]
    label_width = labels.shape[2]
    frames_before, frames_after = frame_halo(inputs[0], half_width)
    padded = jnp.concatenate([frames_before, inputs[0], frames_after], axis=0)
    before = rec_span[0, 0]
    after = rec_span[1, 0]
    pieces = []
    for tap_index in range(tap_count):
        offset = tap_index - half_width
        shifted = padded[tap_index : tap_index + shard_rows]
        if offset < 0:
            shifted = jnp.where((before >= -offset)[:, None], shifted, jnp.zeros_like(shifted))
        elif offset > 0:
            shifted = jnp.where((after >= offset)[:, None], shifted, jnp.zeros_like(shifted))
        pieces.append(shifted)
    stacked = jnp.concatenate(pieces, axis=1)
    flat_weight = conv_weight.reshape(tap_count * conv_weight.shape[1], feat_width)
    pre_act = jnp.dot(stacked, flat_weight, preferred_element_type=jnp.float32) + conv_bias
    features = jax.nn.gelu(pre_act, approximate=False).astype(jnp.bfloat16)
    joined = jnp.concatenate([features, labels[0].astype(jnp.bfloat16)], axis=1)
    moments = lax.dot_general(
        features, joined, (((0,), (0,)), ((), ())), preferred_element_type=jnp.float32
    )
    totals = jnp.sum(joined, axis=0, dtype=jnp.float32)

    row_blocks = feat_width // BLOCK
    col_blocks = row_blocks + label_width // BLOCK
    kept = [(i, j) for i in range(row_blocks) for j in range(i, col_blocks)]
    blocks = [
        moments[i * BLOCK : (i + 1) * BLOCK, j * BLOCK : (j + 1) * BLOCK] for i, j in kept
    ]
    total_rows = totals.reshape(-1, BLOCK)
    blocks.append(jnp.pad(total_rows, ((0, BLOCK - total_rows.shape[0]), (0, 0))))
    if len(blocks) % 2:
        blocks.append(jnp.zeros((BLOCK, BLOCK), jnp.float32))
    payload = jnp.concatenate(blocks, axis=0).reshape(2, -1, BLOCK)
    mine, other = all_sum(payload)
    frame_count = lax.axis_size(("x", "z", "y", "core")) * inputs.shape[0] * shard_rows
    probe_weights = ridge_solve(mine, other, kept, row_blocks, col_blocks, frame_count)
    return (features[None], probe_weights)


def solution(mesh):
    physical = Mesh(mesh.devices.reshape(4, 8, 4, 2), ("x", "z", "y", "core"))
    frame, rec = ("x", "z"), ("y", "core")
    in_specs = (P(rec, frame, None), P(), P(), P(rec, frame, None), P(None, rec, frame))
    out_specs = (P(rec, frame, None), P())
    return jax.shard_map(
        per_device, mesh=physical, in_specs=in_specs, out_specs=out_specs, check_vma=False
    )
```

profile of v0, /device:TPU:1, one launch (start us, length us, event | category | flops | bytes accessed | tf_op | source)
XLA Modules:
  0.0 117.1 jit_solution(14927926414823658454)
XLA Ops:
  0.6 0.0 copy-start
  0.6 0.9 slice_bitcast_fusion
  1.5 4.4 %collective-permute-start = (bf16[2,512]{1,0:T(2,128)(2,1)S(1)}, bf16[2,512]{1,0:T(2,128)(2,1)S(1)}, u32[]{:S(2)}, u32[]{:S(2)}) collective-permute-start(bf16[2,512]{1,0:T(2,128)(2,1)S(1)} %get-tuple-element.33), channel_id=1, source_target_pairs={{0,8},{8,16},{16,24},{24,32},{32,40},{40,48},{48,56},{56,64},{64,7... | collective-permute-start | bytes 6152 | tf_op jit(solution)/shard_map/ppermute | solution.py:20
  5.9 1.3 %collective-permute-start.1 = (bf16[2,512]{1,0:T(2,128)(2,1)S(1)}, bf16[2,512]{1,0:T(2,128)(2,1)S(1)}, u32[]{:S(2)}, u32[]{:S(2)}) collective-permute-start(bf16[2,512]{1,0:T(2,128)(2,1)S(1)} %get-tuple-element.32), channel_id=1, source_target_pairs={{8,0},{16,8},{24,16},{32,24},{40,32},{48,40},{56,48},{64,56},{72,6... | collective-permute-start | bytes 6152 | tf_op jit(solution)/shard_map/ppermute | solution.py:21
  7.2 2.9 %copy.7 = s32[1,1024,512]{1,2,0:T(8,128)} copy(s32[1,1024,512]{2,1,0:T(8,128)} %param.8) | data formatting | bytes 4194304 | tf_op args[3]
  10.1 0.0 copy-start.4
  10.1 2.8 %convert_bitcast_fusion = bf16[1024,512]{0,1:T(8,128)(2,1)} fusion(s32[1,1024,512]{1,2,0:T(8,128)} %copy.7), kind=kLoop, calls=%fused_computation.38 | loop fusion | flops 524288 | bytes 3145728 | tf_op jit(solution)/shard_map/convert_element_type | solution.py:214
  12.9 0.0 copy-done.4
  12.9 0.1 compare_reduce_fusion
  13.0 0.0 copy-start.1
  13.0 0.0 collective-permute-done
  13.0 1.7 %fusion.16 = bf16[1024,2560]{1,0:T(8,128)(2,1)S(1)} fusion(bf16[2,512]{1,0:T(2,128)(2,1)S(1)} %collective-permute-done, bf16[1024,512]{1,0:T(8,128)(2,1)} %bitcast.20, pred[1024]{0:T(1024)(128)(4,1)S(1)} %get-tuple-element.7), kind=kLoop, calls=%fused_computation.31 | loop fusion | flops 2621439 | bytes 2100224
  14.7 0.0 copy-done.1
  14.7 0.3 fusion.20
  15.1 0.1 constant_dynamic-update-slice_fusion
  15.1 0.0 collective-permute-done.1
  15.1 0.0 copy-start.5
  15.2 0.3 fusion.13
  15.5 0.3 fusion.18
  15.9 0.0 copy-done
  15.9 0.0 copy-done.5
  15.9 0.0 copy-start.2
  15.9 7.5 %fusion.2 = bf16[1024,512]{0,1:T(8,128)(2,1)S(1)} fusion(bf16[1024,2560]{1,0:T(8,128)(2,1)S(1)} %fusion.18, bf16[2560,512]{1,0:T(8,128)(2,1)S(1)} %bitcast.17, f32[512]{0:T(512)S(1)} %copy-done.5), kind=kOutput, calls=%fused_computation.4 | convolution fusion | flops 2718957568 | bytes 8914944 | tf_op jit(solution)/shard_map/dot_general | solution.py:212
  23.4 0.0 copy-done.2
  23.5 0.0 copy-start.3
  23.5 1.3 %fusion.10 = f32[512,1024]{1,0:T(8,128)S(1)} fusion(bf16[1024,512]{0,1:T(8,128)(2,1)S(1)} %fusion.2, bf16[1024,512]{0,1:T(8,128)(2,1)S(1)} %copy-done.2), kind=kOutput, calls=%fused_computation.21 | convolution fusion | flops 1077936128 | bytes 4194304 | tf_op jit(solution)/shard_map/dot_general | solution.py:215
  24.8 0.0 copy-done.3
  24.8 0.3 convert_reduce_fusion
  25.4 0.1 broadcast_select_fusion
  25.5 1.0 collective-permute-start.2
  26.6 2.1 %collective-permute-done.2 = f32[1792,128]{1,0:T(8,128)S(1)} collective-permute-done((f32[1792,128]{1,0:T(8,128)S(1)}, f32[1792,128]{1,0:T(8,128)S(1)}, u32[]{:S(2)}, u32[]{:S(2)}) %collective-permute-start.2) | collective-permute-done | bytes 917536 | tf_op jit(solution)/shard_map/ppermute | solution.py:30
  28.7 0.1 select_add_fusion
  28.8 25.2 %all_to_all.10 = f32[16,112,128]{2,1,0:T(8,128)S(1)} all-to-all(f32[16,112,128]{2,1,0:T(8,128)S(1)} %bitcast.25), channel_id=1, replica_groups=mesh['x'=4,'z'=8,'y'=4,'core'=2] {'x','y'}, dimensions={0} | all-to-all | bytes 1835008 | tf_op jit(solution)/shard_map/all_to_all | solution.py:33
  54.0 0.7 reduce_sum.19
  54.7 0.0 collective-permute-start.3
  54.7 3.2 %collective-permute-done.3 = f32[112,128]{1,0:T(8,128)S(1)} collective-permute-done((f32[112,128]{1,0:T(8,128)}, f32[112,128]{1,0:T(8,128)S(1)}, u32[]{:S(2)}, u32[]{:S(2)}) %collective-permute-start.3) | collective-permute-done | bytes 57376 | tf_op jit(solution)/shard_map/ppermute | solution.py:38
  57.9 0.8 add.25
  58.8 0.4 collective-permute-start.4
  59.2 3.8 %collective-permute-done.4 = f32[112,128]{1,0:T(8,128)S(1)} collective-permute-done((f32[112,128]{1,0:T(8,128)S(1)}, f32[112,128]{1,0:T(8,128)S(1)}, u32[]{:S(2)}, u32[]{:S(2)}) %collective-permute-start.4) | collective-permute-done | bytes 57376 | tf_op jit(solution)/shard_map/ppermute | solution.py:38
  63.0 4.4 %collective-permute-start.5 = (f32[112,128]{1,0:T(8,128)S(1)}, f32[112,128]{1,0:T(8,128)S(1)}, u32[]{:S(2)}, u32[]{:S(2)}) collective-permute-start(f32[112,128]{1,0:T(8,128)S(1)} %add.26), channel_id=1, source_target_pairs={{0,32},{8,40},{16,48},{24,56},{32,0},{40,8},{48,16},{56,24},{1,33}... | collective-permute-start | bytes 172040 | tf_op jit(solution)/shard_map/ppermute | solution.py:38
  67.4 2.7 %collective-permute-done.5 = f32[112,128]{1,0:T(8,128)S(1)} collective-permute-done((f32[112,128]{1,0:T(8,128)S(1)}, f32[112,128]{1,0:T(8,128)S(1)}, u32[]{:S(2)}, u32[]{:S(2)}) %collective-permute-start.5) | collective-permute-done | bytes 57376 | tf_op jit(solution)/shard_map/ppermute | solution.py:38
  70.1 0.1 broadcast_in_dim.50
  70.1 14.8 %all_to_all.11 = f32[16,112,128]{2,1,0:T(8,128)S(1)} all-to-all(f32[16,112,128]{2,1,0:T(8,128)S(1)} %broadcast_in_dim.50), channel_id=1, replica_groups=mesh['x'=4,'z'=8,'y'=4,'core'=2] {'x','y'}, dimensions={0} | all-to-all | bytes 1835008 | tf_op jit(solution)/shard_map/all_to_all | solution.py:42
  85.0 6.1 %collective-permute-start.6 = (f32[1792,128]{1,0:T(8,128)S(1)}, f32[1792,128]{1,0:T(8,128)}, u32[]{:S(2)}, u32[]{:S(2)}) collective-permute-start(f32[1792,128]{1,0:T(8,128)S(1)} %bitcast.18), channel_id=1, source_target_pairs={{0,1},{1,0},{2,3},{3,2},{4,5},{5,4},{6,7},{7,6},{8,9},{9,8},{10,11... | collective-permute-start | bytes 2752520 | tf_op jit(solution)/shard_map/ppermute | solution.py:44
  91.1 2.3 %copy.8 = bf16[1,1024,512]{2,1,0:T(8,128)(2,1)} copy(bf16[1,1024,512]{1,2,0:T(8,128)(2,1)} %bitcast.24) | data formatting | bytes 2097152
  93.3 0.0 collective-permute-done.6.other_ref
  93.3 23.8 %ridge_solve.1 = f32[512,512]{1,0:T(8,128)} custom-call(s32[1]{0:T(128)} %bitcast.5.core_ref, f32[1792,128]{1,0:T(8,128)S(1)} %bitcast.19, f32[1792,128]{1,0:T(8,128)} %collective-permute-done.6.other_ref), custom_call_target="tpu_custom_call" | custom-call | tf_op jit(solution)/shard_map/ridge_solve/pallas_call | solution.py:174
  (18 shorter events, 0.2 us)
Async XLA Ops:
  0.6 15.2 %copy-start = (bf16[5,512,512]{2,1,0:T(8,128)(2,1)S(1)}, bf16[5,512,512]{2,1,0:T(8,128)(2,1)}, u32[]{:S(2)}) copy-start(bf16[5,512,512]{2,1,0:T(8,128)(2,1)} %param.6) | copy-start | bytes 7864324
  1.5 11.5 %collective-permute-start = (bf16[2,512]{1,0:T(2,128)(2,1)S(1)}, bf16[2,512]{1,0:T(2,128)(2,1)S(1)}, u32[]{:S(2)}, u32[]{:S(2)}) collective-permute-start(bf16[2,512]{1,0:T(2,128)(2,1)S(1)} %get-tuple-element.33), channel_id=1, source_target_pairs={{0,8},{8,16},{16,24},{24,32},{32,40},{40,48},{48,56},{56,64},{64,7... | collective-permute-start | bytes 6152 | tf_op jit(solution)/shard_map/ppermute | solution.py:20
  5.9 9.3 %collective-permute-start.1 = (bf16[2,512]{1,0:T(2,128)(2,1)S(1)}, bf16[2,512]{1,0:T(2,128)(2,1)S(1)}, u32[]{:S(2)}, u32[]{:S(2)}) collective-permute-start(bf16[2,512]{1,0:T(2,128)(2,1)S(1)} %get-tuple-element.32), channel_id=1, source_target_pairs={{8,0},{16,8},{24,16},{32,24},{40,32},{48,40},{56,48},{64,56},{72,6... | collective-permute-start | bytes 6152 | tf_op jit(solution)/shard_map/ppermute | solution.py:21
  10.1 2.8 %copy-start.4 = (s32[2,1,1024]{2,1,0:T(1,128)S(1)}, s32[2,1,1024]{2,1,0:T(1,128)}, u32[]{:S(2)}) copy-start(s32[2,1,1024]{2,1,0:T(1,128)} %param.9) | copy-start | bytes 24580
  13.0 1.7 %copy-start.1 = (bf16[1,1024,512]{2,1,0:T(8,128)(2,1)S(1)}, bf16[1,1024,512]{2,1,0:T(8,128)(2,1)}, u32[]{:S(2)}) copy-start(bf16[1,1024,512]{2,1,0:T(8,128)(2,1)} %param.5) | copy-start | bytes 3145732
  15.1 0.7 copy-start.5
  15.9 7.6 %copy-start.2 = (bf16[1024,512]{0,1:T(8,128)(2,1)S(1)}, bf16[1024,512]{0,1:T(8,128)(2,1)}, u32[]{:S(2)}) copy-start(bf16[1024,512]{0,1:T(8,128)(2,1)} %convert_bitcast_fusion) | copy-start | bytes 3145732
  23.5 1.3 %copy-start.3 = (bf16[1024,512]{0,1:T(8,128)(2,1)}, bf16[1024,512]{0,1:T(8,128)(2,1)S(1)}, u32[]{:S(2)}) copy-start(bf16[1024,512]{0,1:T(8,128)(2,1)S(1)} %fusion.2) | copy-start | bytes 3145732
  25.5 3.1 %collective-permute-start.2 = (f32[1792,128]{1,0:T(8,128)S(1)}, f32[1792,128]{1,0:T(8,128)S(1)}, u32[]{:S(2)}, u32[]{:S(2)}) collective-permute-start(f32[1792,128]{1,0:T(8,128)S(1)} %broadcast_select_fusion), channel_id=1, source_target_pairs={{0,1},{1,0},{2,3},{3,2},{4,5},{5,4},{6,7},{7,6},{8,9},{9,8},{10,11... | collective-permute-start | bytes 2752520 | tf_op jit(solution)/shard_map/ppermute | solution.py:30
  54.7 3.2 %collective-permute-start.3 = (f32[112,128]{1,0:T(8,128)}, f32[112,128]{1,0:T(8,128)S(1)}, u32[]{:S(2)}, u32[]{:S(2)}) collective-permute-start(f32[112,128]{1,0:T(8,128)} %reduce_sum.19), channel_id=1, source_target_pairs={{0,8},{8,0},{16,24},{24,16},{32,40},{40,32},{48,56},{56,48},{1,9},... | collective-permute-start | bytes 172040 | tf_op jit(solution)/shard_map/ppermute | solution.py:38
  58.8 4.3 %collective-permute-start.4 = (f32[112,128]{1,0:T(8,128)S(1)}, f32[112,128]{1,0:T(8,128)S(1)}, u32[]{:S(2)}, u32[]{:S(2)}) collective-permute-start(f32[112,128]{1,0:T(8,128)S(1)} %add.25), channel_id=1, source_target_pairs={{0,16},{8,24},{16,0},{24,8},{32,48},{40,56},{48,32},{56,40},{1,17}... | collective-permute-start | bytes 172040 | tf_op jit(solution)/shard_map/ppermute | solution.py:38
  63.0 7.0 %collective-permute-start.5 = (f32[112,128]{1,0:T(8,128)S(1)}, f32[112,128]{1,0:T(8,128)S(1)}, u32[]{:S(2)}, u32[]{:S(2)}) collective-permute-start(f32[112,128]{1,0:T(8,128)S(1)} %add.26), channel_id=1, source_target_pairs={{0,32},{8,40},{16,48},{24,56},{32,0},{40,8},{48,16},{56,24},{1,33}... | collective-permute-start | bytes 172040 | tf_op jit(solution)/shard_map/ppermute | solution.py:38
  85.0 8.4 %collective-permute-start.6 = (f32[1792,128]{1,0:T(8,128)S(1)}, f32[1792,128]{1,0:T(8,128)}, u32[]{:S(2)}, u32[]{:S(2)}) collective-permute-start(f32[1792,128]{1,0:T(8,128)S(1)} %bitcast.18), channel_id=1, source_target_pairs={{0,1},{1,0},{2,3},{3,2},{4,5},{5,4},{6,7},{7,6},{8,9},{9,8},{10,11... | collective-permute-start | bytes 2752520 | tf_op jit(solution)/shard_map/ppermute | solution.py:44
where the time goes:
time: 118 us; the launch traced here: 117 us
  blocking collectives  40 us (34%)
  Pallas kernels  23.8 us (20%)
  starting transfers between devices  17.6 us (15%)
  waiting for transfers between devices  11.8 us (10%)
  matrix products  8.84 us (7%)
  other arithmetic  7.65 us (6%)
  local copies, waits for them, and re-layouts  6.43 us (5%)
    all_to_all x1, blocking collectives, all_sum(): lax.all_to_all(part.reshape(peers, rows, BLOCK), ('x', 'y'), split_axis=0...  25.2 us
    pallas_call x1, Pallas kernels, ridge_solve(): pl.pallas_call(functools.partial(solve_kernel, kept, row_blocks, col_bloc...  23.8 us
    all_to_all x1, blocking collectives, all_sum(): lax.all_to_all(spread, ('x', 'y'), split_axis=0, concat_axis=0, tiled=True)  14.8 us
    ppermute x3, waiting for transfers between devices, all_sum(): lax.ppermute(chunk, 'z', [(i, i ^ bit) for i in range(lax.axis_size('z'))])  9.72 us
    dot_general x1, matrix products, per_device(): jnp.dot(stacked, flat_weight, preferred_element_type=jnp.float32)  7.55 us
    ppermute x1, starting transfers between devices, all_sum(): other = lax.ppermute(mine, 'core', swap)  6.11 us
    unnamed x29, local copies, waits for them, and re-layouts  5.47 us
    ppermute x3, starting transfers between devices, all_sum(): lax.ppermute(chunk, 'z', [(i, i ^ bit) for i in range(lax.axis_size('z'))])  4.8 us
  transfers between devices with their start and end apart: 7, of which 4 were waited for; matrix products, arithmetic and copies ran while one was open for 9% of the time, Pallas kernels for 0%

commit v1 on v0

--- a/solution.py
+++ b/solution.py
@@ -11,6 +11,11 @@
 RIDGE = 0.1
 BLOCK = 128
 GROUP = 8
+TAP_REACH = 2
+PAD = 8
+EDGE = 16
+ROWS = 256
+VMEM = 56 * 1024 * 1024
 
 
 def frame_halo(rows, width):
@@ -22,11 +27,8 @@
     return before, after
 
 
-def all_sum(halves):
-    core = lax.axis_index("core")
+def all_sum(keep, send):
     swap = [(0, 1), (1, 0)]
-    keep = jnp.where(core == 0, halves[0], halves[1])
-    send = jnp.where(core == 0, halves[1], halves[0])
     part = keep + lax.ppermute(send, "core", swap)
     peers = lax.axis_size(("x", "y"))
     rows = part.shape[0] // peers
@@ -43,6 +45,130 @@
     mine = full.reshape(peers * rows, BLOCK)
     other = lax.ppermute(mine, "core", swap)
     return mine, other
+
+
+def gelu(value):
+    return 0.5 * value * (1.0 + lax.erf(value * math.sqrt(0.5)))
+
+
+def frames_code(span):
+    before = jnp.minimum(span[0], TAP_REACH)
+    after = jnp.minimum(span[1], TAP_REACH)
+    return (before + (TAP_REACH + 1) * after).astype(jnp.float32)
+
+
+def tap_masks(code, width):
+    code = jnp.concatenate([code] * (width // BLOCK), axis=1)
+    after = jnp.floor(code * (1.0 / (TAP_REACH + 1)) + 0.01)
+    before = code - (TAP_REACH + 1) * after
+    masks = {0: None}
+    for far in range(1, TAP_REACH + 1):
+        masks[-far] = before >= far - 0.5
+        masks[far] = after >= far - 0.5
+    return masks
+
+
+def down_lanes(code_row):
+    return jnp.broadcast_to(code_row, (BLOCK, BLOCK)).T
+
+
+def features_of(taps_ref, rows, weight_ref, bias_ref):
+    pre_act = jnp.dot(taps_ref[rows, :], weight_ref[...], preferred_element_type=jnp.float32)
+    return gelu(pre_act + bias_ref[...]).astype(jnp.bfloat16)
+
+
+def conv_kernel(inputs_ref, weight_ref, bias_ref, labels_ref, code_ref, joined_ref, wide, taps):
+    frames, width = inputs_ref.shape
+    feats = weight_ref.shape[1]
+    wide[0:PAD, :] = jnp.zeros((PAD, width), jnp.float32)
+    wide[PAD + frames :, :] = jnp.zeros((PAD, width), jnp.float32)
+    wide[PAD : PAD + frames, :] = inputs_ref[...].astype(jnp.float32)
+    for first in range(0, frames, ROWS):
+        for start in range(first, first + ROWS, BLOCK):
+            at = slice(start, start + BLOCK)
+            masks = tap_masks(down_lanes(code_ref[start // BLOCK : start // BLOCK + 1, :]), width)
+            for tap, offset in enumerate(range(-TAP_REACH, TAP_REACH + 1)):
+                columns = slice(tap * width, (tap + 1) * width)
+                if offset == 0:
+                    taps[at, columns] = inputs_ref[at, :]
+                else:
+                    shifted = wide[PAD + start + offset : PAD + start + offset + BLOCK, :]
+                    taps[at, columns] = jnp.where(masks[offset], shifted, 0.0).astype(jnp.bfloat16)
+        rows = slice(first, first + ROWS)
+        joined_ref[rows, feats:] = labels_ref[rows, :].astype(jnp.float32).astype(jnp.bfloat16)
+        joined_ref[rows, :feats] = features_of(taps, rows, weight_ref, bias_ref)
+
+
+def moments_kernel(
+    kept, core_ref, joined_ref, inputs_ref, halo_ref, weight_ref, bias_ref, code_ref,
+    features_ref, keep_ref, send_ref, joined, edges, taps, blocks, sems,
+):
+    frames, width = inputs_ref.shape
+    feats = weight_ref.shape[1]
+    last = frames - EDGE
+    edges[0, 0:PAD, :] = jnp.concatenate(
+        [jnp.zeros((PAD - TAP_REACH, width), jnp.float32), halo_ref[0:TAP_REACH, :].astype(jnp.float32)], axis=0
+    )
+    edges[0, PAD:, :] = inputs_ref[0 : EDGE + PAD, :].astype(jnp.float32)
+    edges[1, 0 : EDGE + PAD, :] = inputs_ref[last - PAD :, :].astype(jnp.float32)
+    edges[1, EDGE + PAD :, :] = jnp.concatenate(
+        [halo_ref[TAP_REACH:, :].astype(jnp.float32), jnp.zeros((PAD - TAP_REACH, width), jnp.float32)], axis=0
+    )
+    for side, first in enumerate((0, last)):
+        block = first // BLOCK
+        code = down_lanes(code_ref[block : block + 1, :])[first % BLOCK : first % BLOCK + EDGE]
+        masks = tap_masks(code, width)
+        at = slice(side * EDGE, (side + 1) * EDGE)
+        for tap, offset in enumerate(range(-TAP_REACH, TAP_REACH + 1)):
+            shifted = edges[side, PAD + offset : PAD + offset + EDGE, :]
+            if offset:
+                shifted = jnp.where(masks[offset], shifted, 0.0)
+            taps[at, tap * width : (tap + 1) * width] = shifted.astype(jnp.bfloat16)
+    joined[...] = joined_ref[...]
+    edge_features = features_of(taps, slice(None), weight_ref, bias_ref)
+    joined[0:EDGE, :feats] = edge_features[:EDGE]
+    joined[last:, :feats] = edge_features[EDGE:]
+    features_ref[...] = joined[:, :feats]
+
+    totals = jnp.dot(
+        jnp.ones((16, frames), jnp.bfloat16), joined[...], preferred_element_type=jnp.float32
+    )[0:1]
+    row_blocks = feats // BLOCK
+    lane = lax.broadcasted_iota(jnp.int32, (8, BLOCK), 1)
+    zero_rows = jnp.zeros((4, BLOCK), jnp.float32)
+    half = blocks.shape[1] // BLOCK
+    places = {pair: divmod(n, half) for n, pair in enumerate(kept)}
+    for first in range(0, row_blocks, 2):
+        left = joined[:, first * BLOCK : (first + 2) * BLOCK]
+        right = joined[:, first * BLOCK :]
+        moments = lax.dot_general(
+            left, right, (((0,), (0,)), ((), ())), preferred_element_type=jnp.float32
+        )
+        for i in (first, first + 1):
+            for j in range(i, joined.shape[1] // BLOCK):
+                owner, place = places[i, j]
+                block = moments[
+                    (i - first) * BLOCK : (i - first + 1) * BLOCK,
+                    (j - first) * BLOCK : (j - first + 1) * BLOCK,
+                ]
+                blocks[owner, place * BLOCK : (place + 1) * BLOCK, :] = block
+                if i == j:
+                    pair = [totals[:, n * BLOCK : (n + 1) * BLOCK] for n in (i, i + row_blocks)]
+                    rows = [row for t in pair for row in (t, pltpu.roll(t, BLOCK // 2, 1))]
+                    middle = BLOCK // 2
+                    spot = slice(place * BLOCK + middle, place * BLOCK + middle + 8)
+                    blocks[owner, spot, :] = jnp.where(
+                        lane < middle, jnp.concatenate(rows + [zero_rows], axis=0), block[middle : middle + 8]
+                    )
+    core = core_ref[0]
+    copies = [
+        pltpu.make_async_copy(blocks.at[core], keep_ref, sems.at[0]),
+        pltpu.make_async_copy(blocks.at[1 - core], send_ref, sems.at[1]),
+    ]
+    for copy in copies:
+        copy.start()
+    for copy in copies:
+        copy.wait()
 
 
 def group_inverse(diag, rows):
@@ -141,14 +267,30 @@
     def span(i, j=None):
         return slice(i * BLOCK, (i + 1 if j is None else j) * BLOCK)
 
-    totals = summed(len(kept))[:col_blocks]
     diagonal = lax.broadcasted_iota(jnp.int32, (BLOCK, BLOCK), 0) == lax.broadcasted_iota(
         jnp.int32, (BLOCK, BLOCK), 1
     )
-    across = [jnp.broadcast_to(totals[j : j + 1], (BLOCK, BLOCK)) for j in range(col_blocks)]
+    middle = BLOCK // 2
+    lane = lax.broadcasted_iota(jnp.int32, (1, BLOCK), 1)
+    wanted = (lax.broadcasted_iota(jnp.int32, (BLOCK, BLOCK), 0) < middle) | (
+        lax.broadcasted_iota(jnp.int32, (BLOCK, BLOCK), 1) >= middle
+    )
+    across = [None] * col_blocks
+    squares = []
+    for i in range(row_blocks):
+        square = summed(kept.index((i, i)))
+        riding = square[middle : middle + 8]
+        for n, j in enumerate((i, i + row_blocks)):
+            total = jnp.where(
+                lane < middle,
+                riding[2 * n : 2 * n + 1],
+                pltpu.roll(riding[2 * n + 1 : 2 * n + 2], middle, 1),
+            )
+            across[j] = jnp.broadcast_to(total, (BLOCK, BLOCK))
+        squares.append(jnp.where(wanted, square, square.T))
     down = [across[i].T for i in range(row_blocks)]
     for n, (i, j) in enumerate(kept):
-        centred = summed(n) - down[i] * across[j] / frame_count
+        centred = (squares[i] if i == j else summed(n)) - down[i] * across[j] / frame_count
         if j >= row_blocks:
             work[span(i), span(j)] = centred / math.sqrt(frame_count)
         else:
@@ -183,53 +325,60 @@
         ],
         out_specs=pl.BlockSpec(memory_space=pltpu.VMEM),
         scratch_shapes=[pltpu.VMEM((row_blocks * BLOCK, col_blocks * BLOCK), jnp.float32)],
-        compiler_params=pltpu.CompilerParams(vmem_limit_bytes=40 * 1024 * 1024),
+        compiler_params=pltpu.CompilerParams(vmem_limit_bytes=VMEM),
         name="ridge_solve",
     )(core, mine, other)
 
 
 def per_device(inputs, conv_weight, conv_bias, labels, rec_span):
-    tap_count = conv_weight.shape[0]
-    half_width = tap_count // 2
-    shard_rows = inputs.shape[1]
-    feat_width = conv_weight.shape[2]
+    frames, width = inputs.shape[1:]
+    feats = conv_weight.shape[2]
     label_width = labels.shape[2]
-    frames_before, frames_after = frame_halo(inputs[0], half_width)
-    padded = jnp.concatenate([frames_before, inputs[0], frames_after], axis=0)
-    before = rec_span[0, 0]
-    after = rec_span[1, 0]
-    pieces = []
-    for tap_index in range(tap_count):
-        offset = tap_index - half_width
-        shifted = padded[tap_index : tap_index + shard_rows]
-        if offset < 0:
-            shifted = jnp.where((before >= -offset)[:, None], shifted, jnp.zeros_like(shifted))
-        elif offset > 0:
-            shifted = jnp.where((after >= offset)[:, None], shifted, jnp.zeros_like(shifted))
-        pieces.append(shifted)
-    stacked = jnp.concatenate(pieces, axis=1)
-    flat_weight = conv_weight.reshape(tap_count * conv_weight.shape[1], feat_width)
-    pre_act = jnp.dot(stacked, flat_weight, preferred_element_type=jnp.float32) + conv_bias
-    features = jax.nn.gelu(pre_act, approximate=False).astype(jnp.bfloat16)
-    joined = jnp.concatenate([features, labels[0].astype(jnp.bfloat16)], axis=1)
-    moments = lax.dot_general(
-        features, joined, (((0,), (0,)), ((), ())), preferred_element_type=jnp.float32
-    )
-    totals = jnp.sum(joined, axis=0, dtype=jnp.float32)
-
-    row_blocks = feat_width // BLOCK
+    rows = inputs[0]
+    halo = jnp.concatenate(frame_halo(rows, TAP_REACH), axis=0)
+    weight = conv_weight.reshape(-1, feats)
+    bias = conv_bias[None]
+    code = frames_code(rec_span[:, 0].reshape(2, -1, BLOCK))
+    core = lax.axis_index("core").astype(jnp.int32)[None]
+    row_blocks = feats // BLOCK
     col_blocks = row_blocks + label_width // BLOCK
     kept = [(i, j) for i in range(row_blocks) for j in range(i, col_blocks)]
-    blocks = [
-        moments[i * BLOCK : (i + 1) * BLOCK, j * BLOCK : (j + 1) * BLOCK] for i, j in kept
-    ]
-    total_rows = totals.reshape(-1, BLOCK)
-    blocks.append(jnp.pad(total_rows, ((0, BLOCK - total_rows.shape[0]), (0, 0))))
-    if len(blocks) % 2:
-        blocks.append(jnp.zeros((BLOCK, BLOCK), jnp.float32))
-    payload = jnp.concatenate(blocks, axis=0).reshape(2, -1, BLOCK)
-    mine, other = all_sum(payload)
-    frame_count = lax.axis_size(("x", "z", "y", "core")) * inputs.shape[0] * shard_rows
+    params = pltpu.CompilerParams(vmem_limit_bytes=VMEM)
+    vmem = pl.BlockSpec(memory_space=pltpu.VMEM)
+    smem = pl.BlockSpec(memory_space=pltpu.SMEM)
+    anywhere = pl.BlockSpec(memory_space=pl.ANY)
+    flops = 2 * frames * weight.shape[0] * feats
+    joined = pl.pallas_call(
+        conv_kernel,
+        out_shape=jax.ShapeDtypeStruct((frames, feats + label_width), jnp.bfloat16),
+        in_specs=[vmem] * 5,
+        out_specs=vmem,
+        scratch_shapes=[
+            pltpu.VMEM((frames + 2 * PAD, width), jnp.float32),
+            pltpu.VMEM((frames, weight.shape[0]), jnp.bfloat16),
+        ],
+        compiler_params=params,
+        cost_estimate=pl.CostEstimate(flops=flops, bytes_accessed=8 << 20, transcendentals=0),
+        name="conv_gelu",
+    )(rows, weight, bias, labels[0], code)
+    half = jax.ShapeDtypeStruct((len(kept) // 2 * BLOCK, BLOCK), jnp.float32)
+    features, keep, send = pl.pallas_call(
+        functools.partial(moments_kernel, kept),
+        out_shape=[jax.ShapeDtypeStruct((frames, feats), jnp.bfloat16), half, half],
+        in_specs=[smem] + [vmem] * 6,
+        out_specs=[vmem, anywhere, anywhere],
+        scratch_shapes=[
+            pltpu.VMEM((frames, feats + label_width), jnp.bfloat16),
+            pltpu.VMEM((2, EDGE + 2 * PAD, width), jnp.float32),
+            pltpu.VMEM((2 * EDGE, weight.shape[0]), jnp.bfloat16),
+            pltpu.VMEM((2,) + half.shape, jnp.float32),
+            pltpu.SemaphoreType.DMA((2,)),
+        ],
+        compiler_params=params,
+        name="moments",
+    )(core, joined, rows, halo, weight, bias, code)
+    mine, other = all_sum(keep, send)
+    frame_count = lax.axis_size(("x", "z", "y", "core")) * inputs.shape[0] * frames
     probe_weights = ridge_solve(mine, other, kept, row_blocks, col_blocks, frame_count)
     return (features[None], probe_weights)
 

time: 118 us -> 115 us (0.975)
  Pallas kernels: 23.8 us -> 38.8 us
  matrix products: 8.84 us -> 0 us
  local copies, waits for them, and re-layouts: 6.43 us -> 1.72 us
  other arithmetic: 7.65 us -> 3.22 us
  waiting for transfers between devices: 11.8 us -> 13.6 us
    pallas_call x0 -> x2, Pallas kernels: none -> 14.4 us  [the longest x1 7.52 us: per_device(): pl.pallas_call(conv_kernel, out_shape=jax.ShapeDtypeStruct((frames, feats...]
    dot_general x2 -> x0, matrix products: 8.84 us -> none  [the longest x1 7.55 us: per_device(): jnp.dot(stacked, flat_weight, preferred_element_type=jnp.float32)]
    unnamed x29 -> x4, local copies, waits for them, and re-layouts: 5.47 us -> 0.94 us
    unnamed x3 -> x0, other arithmetic: 2.34 us -> none
    ppermute x1, waiting for transfers between devices: 0.01 us -> 2.01 us  [all_sum(): other = lax.ppermute(mine, 'core', swap)]
    convert_element_type x1, other arithmetic: 2.82 us -> 1.31 us  [frames_code(): return (before + (TAP_REACH + 1) * after).astype(jnp.float32)]
  transfers between devices with their start and end apart: 7 -> 7, of which waited for: 4 -> 5; matrix products, arithmetic and copies ran while one was open for 9% -> 1% of each run, Pallas kernels for 0% -> 7%
where the time goes in v1:
time: 115 us
  blocking collectives  39 us (34%)
  Pallas kernels  38.8 us (34%)
  starting transfers between devices  17.8 us (15%)
  waiting for transfers between devices  13.6 us (12%)
  other arithmetic  3.22 us (3%)
  local copies, waits for them, and re-layouts  1.72 us (1%)
    all_to_all x1, blocking collectives, all_sum(): lax.all_to_all(part.reshape(peers, rows, BLOCK), ('x', 'y'), split_axis=0...  24.8 us
    pallas_call x1, Pallas kernels, ridge_solve(): pl.pallas_call(functools.partial(solve_kernel, kept, row_blocks, col_bloc...  24.4 us
    all_to_all x1, blocking collectives, all_sum(): lax.all_to_all(spread, ('x', 'y'), split_axis=0, concat_axis=0, tiled=True)  14.2 us
    ppermute x3, waiting for transfers between devices, all_sum(): lax.ppermute(chunk, 'z', [(i, i ^ bit) for i in range(lax.axis_size('z'))])  9.35 us
    pallas_call x1, Pallas kernels, per_device(): pl.pallas_call(conv_kernel, out_shape=jax.ShapeDtypeStruct((frames, feats...  7.52 us
    pallas_call x1, Pallas kernels, per_device(): pl.pallas_call(functools.partial(moments_kernel, kept), out_shape=[jax.Sh...  6.88 us
    ppermute x1, starting transfers between devices, all_sum(): other = lax.ppermute(mine, 'core', swap)  6.12 us
    ppermute x3, starting transfers between devices, all_sum(): lax.ppermute(chunk, 'z', [(i, i ^ bit) for i in range(lax.axis_size('z'))])  4.96 us
  transfers between devices with their start and end apart: 7, of which 5 were waited for; matrix products, arithmetic and copies ran while one was open for 1% of the time, Pallas kernels for 7%

profile of v1, /device:TPU:1, one launch (start us, length us, event | category | flops | bytes accessed | tf_op | source)
XLA Modules:
  0.0 114.8 jit_solution(15577548939437873372)
XLA Ops:
  0.6 0.7 slice_bitcast_fusion.1
  1.4 4.4 %collective-permute-start = (bf16[2,512]{1,0:T(2,128)(2,1)S(1)}, bf16[2,512]{1,0:T(2,128)(2,1)S(1)}, u32[]{:S(2)}, u32[]{:S(2)}) collective-permute-start(bf16[2,512]{1,0:T(2,128)(2,1)S(1)} %get-tuple-element.8), channel_id=1, source_target_pairs={{0,8},{8,16},{16,24},{24,32},{32,40},{40,48},{48,56},{56,64},{64,7... | collective-permute-start | bytes 6152 | tf_op jit(solution)/shard_map/ppermute | solution.py:25
  5.7 1.3 %collective-permute-start.1 = (bf16[2,512]{1,0:T(2,128)(2,1)S(1)}, bf16[2,512]{1,0:T(2,128)(2,1)S(1)}, u32[]{:S(2)}, u32[]{:S(2)}) collective-permute-start(bf16[2,512]{1,0:T(2,128)(2,1)S(1)} %get-tuple-element.9), channel_id=1, source_target_pairs={{8,0},{16,8},{24,16},{32,24},{40,32},{48,40},{56,48},{64,56},{72,6... | collective-permute-start | bytes 6152 | tf_op jit(solution)/shard_map/ppermute | solution.py:26
  7.0 1.3 %add_convert_fusion = f32[1,1,1024]{2,1,0:T(1,128)} fusion(s32[2,1,1024]{2,1,0:T(1,128)} %param.9), kind=kLoop, calls=%fused_computation.1 | loop fusion | flops 5120 | bytes 12288 | tf_op jit(solution)/shard_map/convert_element_type | solution.py:57
  8.3 7.5 %conv_gelu.1.joined_ref = bf16[1024,1024]{1,0:T(8,128)(2,1)} custom-call(bf16[1024,512]{1,0:T(8,128)(2,1)} %bitcast.18, bf16[2560,512]{1,0:T(8,128)(2,1)} %bitcast.16, f32[1,512]{1,0:T(1,128)} %bitcast.22, s32[1024,512]{1,0:T(8,128)} %bitcast.24, f32[8,128]{1,0:T(8,128)} %bitcast.20), custom_call_target="tpu_custom_call" | custom-call | flops 2684354560 | bytes 8388608 | tf_op jit(solution)/shard_map/conv_gelu/pallas_call | solution.py:351
  15.9 0.0 collective-permute-done
  15.9 0.0 collective-permute-done.1
  15.9 0.6 pad_maximum_fusion.halo_ref
  16.5 6.9 %moments.1 = (bf16[1024,512]{1,0:T(8,128)(2,1)}, f32[1664,128]{1,0:T(8,128)}, f32[1664,128]{1,0:T(8,128)}) custom-call(s32[1]{0:T(128)} %bitcast.core_ref, bf16[1024,1024]{1,0:T(8,128)(2,1)} %conv_gelu.1.joined_ref, bf16[1024,512]{1,0:T(8,128)(2,1)} %bitcast.19, bf16[4,512]{1,0:T(4,128)(2,1)} %pad_maximum_fusion.halo_ref, bf16[2560,512]{1,0:T(8,128)(2,1)} %bitcast.17, ...), custom_call_target="tpu_custom_call" | custom-call | tf_op jit(solution)/shard_map/moments/pallas_call | solution.py:365
  23.3 1.0 collective-permute-start.2
  24.4 2.2 %collective-permute-done.2 = f32[1664,128]{1,0:T(8,128)S(1)} collective-permute-done((f32[1664,128]{1,0:T(8,128)}, f32[1664,128]{1,0:T(8,128)S(1)}, u32[]{:S(2)}, u32[]{:S(2)}) %collective-permute-start.2) | collective-permute-done | bytes 852000 | tf_op jit(solution)/shard_map/ppermute | solution.py:32
  26.6 1.2 %add.17 = f32[1664,128]{1,0:T(8,128)S(1)} add(f32[1664,128]{1,0:T(8,128)} %get-tuple-element.6, f32[1664,128]{1,0:T(8,128)S(1)} %collective-permute-done.2) | non-fusion elementwise | flops 212992 | bytes 2555904 | tf_op jit(solution)/shard_map/add | solution.py:32
  27.8 24.8 %all_to_all.10 = f32[16,104,128]{2,1,0:T(8,128)S(1)} all-to-all(f32[16,104,128]{2,1,0:T(8,128)S(1)} %bitcast.13), channel_id=1, replica_groups=mesh['x'=4,'z'=8,'y'=4,'core'=2] {'x','y'}, dimensions={0} | all-to-all | bytes 1703936 | tf_op jit(solution)/shard_map/all_to_all | solution.py:35
  52.7 0.1 collective-permute-start.3
  52.8 3.0 %collective-permute-done.3 = f32[104,128]{1,0:T(8,128)S(1)} collective-permute-done((f32[104,128]{1,0:T(8,128)S(1)}, f32[104,128]{1,0:T(8,128)S(1)}, u32[]{:S(2)}, u32[]{:S(2)}) %collective-permute-start.3) | collective-permute-done | bytes 53280 | tf_op jit(solution)/shard_map/ppermute | solution.py:40
  55.8 0.5 collective-permute-start.4
  56.3 3.7 %collective-permute-done.4 = f32[104,128]{1,0:T(8,128)S(1)} collective-permute-done((f32[104,128]{1,0:T(8,128)S(1)}, f32[104,128]{1,0:T(8,128)S(1)}, u32[]{:S(2)}, u32[]{:S(2)}) %collective-permute-start.4) | collective-permute-done | bytes 53280 | tf_op jit(solution)/shard_map/ppermute | solution.py:40
  60.1 4.3 %collective-permute-start.5 = (f32[104,128]{1,0:T(8,128)S(1)}, f32[104,128]{1,0:T(8,128)S(1)}, u32[]{:S(2)}, u32[]{:S(2)}) collective-permute-start(f32[104,128]{1,0:T(8,128)S(1)} %add.19), channel_id=1, source_target_pairs={{0,32},{8,40},{16,48},{24,56},{32,0},{40,8},{48,16},{56,24},{1,33}... | collective-permute-start | bytes 159752 | tf_op jit(solution)/shard_map/ppermute | solution.py:40
  64.4 2.6 %collective-permute-done.5 = f32[104,128]{1,0:T(8,128)S(1)} collective-permute-done((f32[104,128]{1,0:T(8,128)S(1)}, f32[104,128]{1,0:T(8,128)S(1)}, u32[]{:S(2)}, u32[]{:S(2)}) %collective-permute-start.5) | collective-permute-done | bytes 53280 | tf_op jit(solution)/shard_map/ppermute | solution.py:40
  67.1 0.1 broadcast_in_dim.19
  67.1 14.2 %all_to_all.11 = f32[16,104,128]{2,1,0:T(8,128)S(1)} all-to-all(f32[16,104,128]{2,1,0:T(8,128)S(1)} %broadcast_in_dim.19), channel_id=1, replica_groups=mesh['x'=4,'z'=8,'y'=4,'core'=2] {'x','y'}, dimensions={0} | all-to-all | bytes 1703936 | tf_op jit(solution)/shard_map/all_to_all | solution.py:44
  81.3 0.0 copy-start
  81.3 6.1 %collective-permute-start.6 = (f32[1664,128]{1,0:T(8,128)S(1)}, f32[1664,128]{1,0:T(8,128)S(1)}, u32[]{:S(2)}, u32[]{:S(2)}) collective-permute-start(f32[1664,128]{1,0:T(8,128)S(1)} %bitcast.14), channel_id=1, source_target_pairs={{0,1},{1,0},{2,3},{3,2},{4,5},{5,4},{6,7},{7,6},{8,9},{9,8},{10,11... | collective-permute-start | bytes 2555912 | tf_op jit(solution)/shard_map/ppermute | solution.py:46
  87.4 2.0 %collective-permute-done.6.other_ref = f32[1664,128]{1,0:T(8,128)S(1)} collective-permute-done((f32[1664,128]{1,0:T(8,128)S(1)}, f32[1664,128]{1,0:T(8,128)S(1)}, u32[]{:S(2)}, u32[]{:S(2)}) %collective-permute-start.6) | collective-permute-done | bytes 852000 | tf_op jit(solution)/shard_map/ppermute | solution.py:46
  89.5 0.0 copy-done
  89.5 0.0 copy-start.1
  89.5 0.9 copy-done.1
  90.4 24.4 %ridge_solve.1 = f32[512,512]{1,0:T(8,128)} custom-call(s32[1]{0:T(128)} %bitcast.core_ref, f32[1664,128]{1,0:T(8,128)} %bitcast.15, f32[1664,128]{1,0:T(8,128)} %copy-done.1), custom_call_target="tpu_custom_call" | custom-call | tf_op jit(solution)/shard_map/ridge_solve/pallas_call | solution.py:316
  (4 shorter events, 0.1 us)
Async XLA Ops:
  1.4 14.5 %collective-permute-start = (bf16[2,512]{1,0:T(2,128)(2,1)S(1)}, bf16[2,512]{1,0:T(2,128)(2,1)S(1)}, u32[]{:S(2)}, u32[]{:S(2)}) collective-permute-start(bf16[2,512]{1,0:T(2,128)(2,1)S(1)} %get-tuple-element.8), channel_id=1, source_target_pairs={{0,8},{8,16},{16,24},{24,32},{32,40},{40,48},{48,56},{56,64},{64,7... | collective-permute-start | bytes 6152 | tf_op jit(solution)/shard_map/ppermute | solution.py:25
  5.7 10.1 %collective-permute-start.1 = (bf16[2,512]{1,0:T(2,128)(2,1)S(1)}, bf16[2,512]{1,0:T(2,128)(2,1)S(1)}, u32[]{:S(2)}, u32[]{:S(2)}) collective-permute-start(bf16[2,512]{1,0:T(2,128)(2,1)S(1)} %get-tuple-element.9), channel_id=1, source_target_pairs={{8,0},{16,8},{24,16},{32,24},{40,32},{48,40},{56,48},{64,56},{72,6... | collective-permute-start | bytes 6152 | tf_op jit(solution)/shard_map/ppermute | solution.py:26
  23.3 3.3 %collective-permute-start.2 = (f32[1664,128]{1,0:T(8,128)}, f32[1664,128]{1,0:T(8,128)S(1)}, u32[]{:S(2)}, u32[]{:S(2)}) collective-permute-start(f32[1664,128]{1,0:T(8,128)} %get-tuple-element.7), channel_id=1, source_target_pairs={{0,1},{1,0},{2,3},{3,2},{4,5},{5,4},{6,7},{7,6},{8,9},{9,8},{10,11... | collective-permute-start | bytes 2555912 | tf_op jit(solution)/shard_map/ppermute | solution.py:32
  52.7 3.1 %collective-permute-start.3 = (f32[104,128]{1,0:T(8,128)S(1)}, f32[104,128]{1,0:T(8,128)S(1)}, u32[]{:S(2)}, u32[]{:S(2)}) collective-permute-start(f32[104,128]{1,0:T(8,128)S(1)} %reduce_sum.9), channel_id=1, source_target_pairs={{0,8},{8,0},{16,24},{24,16},{32,40},{40,32},{48,56},{56,48},{1,9},... | collective-permute-start | bytes 159752 | tf_op jit(solution)/shard_map/ppermute | solution.py:40
  55.8 4.3 %collective-permute-start.4 = (f32[104,128]{1,0:T(8,128)S(1)}, f32[104,128]{1,0:T(8,128)S(1)}, u32[]{:S(2)}, u32[]{:S(2)}) collective-permute-start(f32[104,128]{1,0:T(8,128)S(1)} %add.18), channel_id=1, source_target_pairs={{0,16},{8,24},{16,0},{24,8},{32,48},{40,56},{48,32},{56,40},{1,17}... | collective-permute-start | bytes 159752 | tf_op jit(solution)/shard_map/ppermute | solution.py:40
  60.1 7.0 %collective-permute-start.5 = (f32[104,128]{1,0:T(8,128)S(1)}, f32[104,128]{1,0:T(8,128)S(1)}, u32[]{:S(2)}, u32[]{:S(2)}) collective-permute-start(f32[104,128]{1,0:T(8,128)S(1)} %add.19), channel_id=1, source_target_pairs={{0,32},{8,40},{16,48},{24,56},{32,0},{40,8},{48,16},{56,24},{1,33}... | collective-permute-start | bytes 159752 | tf_op jit(solution)/shard_map/ppermute | solution.py:40
  81.3 8.1 %copy-start = (f32[16,104,128]{2,1,0:T(8,128)}, f32[16,104,128]{2,1,0:T(8,128)S(1)}, u32[]{:S(2)}) copy-start(f32[16,104,128]{2,1,0:T(8,128)S(1)} %all_to_all.11) | copy-start | bytes 2555908
  81.3 8.1 %collective-permute-start.6 = (f32[1664,128]{1,0:T(8,128)S(1)}, f32[1664,128]{1,0:T(8,128)S(1)}, u32[]{:S(2)}, u32[]{:S(2)}) collective-permute-start(f32[1664,128]{1,0:T(8,128)S(1)} %bitcast.14), channel_id=1, source_target_pairs={{0,1},{1,0},{2,3},{3,2},{4,5},{5,4},{6,7},{7,6},{8,9},{9,8},{10,11... | collective-permute-start | bytes 2555912 | tf_op jit(solution)/shard_map/ppermute | solution.py:46
  89.5 0.9 copy-start.1

commit v2 on v0

--- a/solution.py
+++ b/solution.py
@@ -11,6 +11,11 @@
 RIDGE = 0.1
 BLOCK = 128
 GROUP = 8
+TAP_REACH = 2
+PAD = 8
+ROWS = 256
+FRONT_VMEM = 60 * 1024 * 1024
+SOLVE_VMEM = 16 * 1024 * 1024
 
 
 def frame_halo(rows, width):
@@ -22,11 +27,8 @@
     return before, after
 
 
-def all_sum(halves):
-    core = lax.axis_index("core")
+def all_sum(keep, send):
     swap = [(0, 1), (1, 0)]
-    keep = jnp.where(core == 0, halves[0], halves[1])
-    send = jnp.where(core == 0, halves[1], halves[0])
     part = keep + lax.ppermute(send, "core", swap)
     peers = lax.axis_size(("x", "y"))
     rows = part.shape[0] // peers
@@ -34,15 +36,152 @@
         part.reshape(peers, rows, BLOCK), ("x", "y"), split_axis=0, concat_axis=0, tiled=True
     )
     chunk = jnp.sum(chunks, axis=0)
-    for bit in (1, 2, 4):
-        chunk = chunk + lax.ppermute(
-            chunk, "z", [(i, i ^ bit) for i in range(lax.axis_size("z"))]
+    for bits in ((4,), (1, 2, 3)):
+        chunk = chunk + sum(
+            lax.ppermute(chunk, "z", [(i, i ^ bit) for i in range(lax.axis_size("z"))])
+            for bit in bits
         )
     spread = jnp.broadcast_to(chunk[None], (peers, rows, BLOCK))
     full = lax.all_to_all(spread, ("x", "y"), split_axis=0, concat_axis=0, tiled=True)
     mine = full.reshape(peers * rows, BLOCK)
     other = lax.ppermute(mine, "core", swap)
     return mine, other
+
+
+def gelu(value):
+    return 0.5 * value * (1.0 + lax.erf(value * math.sqrt(0.5)))
+
+
+def down_lanes(row):
+    return jnp.broadcast_to(row, (BLOCK, BLOCK)).T
+
+
+def front_kernel(
+    kept, core_ref, inputs_hbm, ahead_hbm, behind_hbm, weight_hbm, bias_hbm, labels_hbm, span_hbm,
+    features_hbm, keep_hbm, send_hbm, inputs, ahead, behind, weight, bias, labels, span,
+    wide, taps, joined, features, halves, sems,
+):
+    frames, width = inputs.shape
+    feats = weight.shape[1]
+    loads = [
+        pltpu.make_async_copy(source, target, sems.at[n])
+        for n, (source, target) in enumerate(
+            (
+                (inputs_hbm, inputs),
+                (ahead_hbm, ahead),
+                (behind_hbm, behind),
+                (span_hbm, span),
+                (bias_hbm, bias),
+                (weight_hbm, weight),
+                (labels_hbm, labels),
+            )
+        )
+    ]
+    for load in loads:
+        load.start()
+    for load in loads[:4]:
+        load.wait()
+    gap = jnp.zeros((PAD - TAP_REACH, width), jnp.float32)
+    wide[0:PAD, :] = jnp.concatenate([gap, ahead[...].astype(jnp.float32)], axis=0)
+    wide[PAD + frames :, :] = jnp.concatenate([behind[...].astype(jnp.float32), gap], axis=0)
+    wide[PAD : PAD + frames, :] = inputs[...].astype(jnp.float32)
+    for start in range(0, frames, BLOCK):
+        at = slice(start, start + BLOCK)
+        line = slice(start // BLOCK, start // BLOCK + 1)
+        spans = [
+            jnp.concatenate([down_lanes(span[side, line, :].astype(jnp.float32))] * (width // BLOCK), axis=1)
+            for side in (0, 1)
+        ]
+        for tap, offset in enumerate(range(-TAP_REACH, TAP_REACH + 1)):
+            columns = slice(tap * width, (tap + 1) * width)
+            if offset == 0:
+                taps[at, columns] = inputs[at, :]
+            else:
+                shifted = wide[PAD + start + offset : PAD + start + offset + BLOCK, :]
+                inside = spans[int(offset > 0)] >= abs(offset) - 0.5
+                taps[at, columns] = jnp.where(inside, shifted, 0.0).astype(jnp.bfloat16)
+    for load in loads[4:6]:
+        load.wait()
+    stores = []
+    for tile, first in enumerate(range(0, frames, ROWS)):
+        rows = slice(first, first + ROWS)
+        pre_act = jnp.dot(taps[rows, :], weight[...], preferred_element_type=jnp.float32)
+        active = gelu(pre_act + bias[...]).astype(jnp.bfloat16)
+        joined[rows, :feats] = active
+        features[rows, :] = active
+        stores.append(
+            pltpu.make_async_copy(features.at[rows], features_hbm.at[rows], sems.at[len(loads) + tile])
+        )
+        stores[-1].start()
+    loads[6].wait()
+    joined[:, feats:] = labels[...].astype(jnp.float32).astype(jnp.bfloat16)
+
+    totals = jnp.dot(
+        jnp.ones((16, frames), jnp.bfloat16), joined[...], preferred_element_type=jnp.float32
+    )[0:1]
+    row_blocks = feats // BLOCK
+    middle = BLOCK // 2
+    lane = lax.broadcasted_iota(jnp.int32, (8, BLOCK), 1)
+    zero_rows = jnp.zeros((4, BLOCK), jnp.float32)
+    half = len(kept) // 2
+    core = core_ref[0]
+
+    for first in range(0, row_blocks, 2):
+        moments = lax.dot_general(
+            joined[:, first * BLOCK : (first + 2) * BLOCK],
+            joined[:, first * BLOCK :],
+            (((0,), (0,)), ((), ())),
+            preferred_element_type=jnp.float32,
+        )
+        for n, (i, j) in enumerate(kept):
+            if i not in (first, first + 1):
+                continue
+            block = moments[
+                (i - first) * BLOCK : (i - first + 1) * BLOCK,
+                (j - first) * BLOCK : (j - first + 1) * BLOCK,
+            ]
+            if i == j:
+                pair = [totals[:, m * BLOCK : (m + 1) * BLOCK] for m in (i, i + row_blocks)]
+                lines = [line for t in pair for line in (t, pltpu.roll(t, middle, 1))]
+                riding = jnp.where(
+                    lane < middle, jnp.concatenate(lines + [zero_rows], axis=0), block[middle : middle + 8]
+                )
+                block = jnp.concatenate([block[:middle], riding, block[middle + 8 :]], axis=0)
+            owner, place = divmod(n, half)
+            halves[owner, place * BLOCK : (place + 1) * BLOCK, :] = block
+    for side, target in ((core, keep_hbm), (1 - core, send_hbm)):
+        stores.append(
+            pltpu.make_async_copy(halves.at[side], target, sems.at[len(loads) + len(stores)])
+        )
+        stores[-1].start()
+    for store in stores:
+        store.wait()
+
+
+def front(core, rows, ahead, behind, weight, bias, labels, span, kept):
+    frames, width = rows.shape
+    feats = weight.shape[1]
+    taps = weight.shape[0]
+    arrays = (rows, ahead, behind, weight, bias, labels, span)
+    hbm = pl.BlockSpec(memory_space=pltpu.HBM)
+    half = jax.ShapeDtypeStruct((len(kept) // 2 * BLOCK, BLOCK), jnp.float32)
+    return pl.pallas_call(
+        functools.partial(front_kernel, kept),
+        out_shape=[jax.ShapeDtypeStruct((frames, feats), jnp.bfloat16), half, half],
+        in_specs=[pl.BlockSpec(memory_space=pltpu.SMEM)] + [hbm] * len(arrays),
+        out_specs=[hbm] * 3,
+        scratch_shapes=[pltpu.VMEM(array.shape, array.dtype) for array in arrays]
+        + [
+            pltpu.VMEM((frames + 2 * PAD, width), jnp.float32),
+            pltpu.VMEM((frames, taps), jnp.bfloat16),
+            pltpu.VMEM((frames, feats + labels.shape[1]), jnp.bfloat16),
+            pltpu.VMEM((frames, feats), jnp.bfloat16),
+            pltpu.VMEM((2,) + half.shape, jnp.float32),
+            pltpu.SemaphoreType.DMA((len(arrays) + frames // ROWS + 2,)),
+        ],
+        compiler_params=pltpu.CompilerParams(vmem_limit_bytes=FRONT_VMEM),
+        name="front",
+    )(core, *arrays)
 
 
 def group_inverse(diag, rows):
@@ -141,14 +280,30 @@
     def span(i, j=None):
         return slice(i * BLOCK, (i + 1 if j is None else j) * BLOCK)
 
-    totals = summed(len(kept))[:col_blocks]
     diagonal = lax.broadcasted_iota(jnp.int32, (BLOCK, BLOCK), 0) == lax.broadcasted_iota(
         jnp.int32, (BLOCK, BLOCK), 1
     )
-    across = [jnp.broadcast_to(totals[j : j + 1], (BLOCK, BLOCK)) for j in range(col_blocks)]
+    middle = BLOCK // 2
+    lane = lax.broadcasted_iota(jnp.int32, (1, BLOCK), 1)
+    wanted = (lax.broadcasted_iota(jnp.int32, (BLOCK, BLOCK), 0) < middle) | (
+        lax.broadcasted_iota(jnp.int32, (BLOCK, BLOCK), 1) >= middle
+    )
+    across = [None] * col_blocks
+    squares = []
+    for i in range(row_blocks):
+        square = summed(kept.index((i, i)))
+        riding = square[middle : middle + 8]
+        for n, j in enumerate((i, i + row_blocks)):
+            total = jnp.where(
+                lane < middle,
+                riding[2 * n : 2 * n + 1],
+                pltpu.roll(riding[2 * n + 1 : 2 * n + 2], middle, 1),
+            )
+            across[j] = jnp.broadcast_to(total, (BLOCK, BLOCK))
+        squares.append(jnp.where(wanted, square, square.T))
     down = [across[i].T for i in range(row_blocks)]
     for n, (i, j) in enumerate(kept):
-        centred = summed(n) - down[i] * across[j] / frame_count
+        centred = (squares[i] if i == j else summed(n)) - down[i] * across[j] / frame_count
         if j >= row_blocks:
             work[span(i), span(j)] = centred / math.sqrt(frame_count)
         else:
@@ -183,53 +338,32 @@
         ],
         out_specs=pl.BlockSpec(memory_space=pltpu.VMEM),
         scratch_shapes=[pltpu.VMEM((row_blocks * BLOCK, col_blocks * BLOCK), jnp.float32)],
-        compiler_params=pltpu.CompilerParams(vmem_limit_bytes=40 * 1024 * 1024),
+        compiler_params=pltpu.CompilerParams(vmem_limit_bytes=SOLVE_VMEM),
         name="ridge_solve",
     )(core, mine, other)
 
 
 def per_device(inputs, conv_weight, conv_bias, labels, rec_span):
-    tap_count = conv_weight.shape[0]
-    half_width = tap_count // 2
-    shard_rows = inputs.shape[1]
-    feat_width = conv_weight.shape[2]
-    label_width = labels.shape[2]
-    frames_before, frames_after = frame_halo(inputs[0], half_width)
-    padded = jnp.concatenate([frames_before, inputs[0], frames_after], axis=0)
-    before = rec_span[0, 0]
-    after = rec_span[1, 0]
-    pieces = []
-    for tap_index in range(tap_count):
-        offset = tap_index - half_width
-        shifted = padded[tap_index : tap_index + shard_rows]
-        if offset < 0:
-            shifted = jnp.where((before >= -offset)[:, None], shifted, jnp.zeros_like(shifted))
-        elif offset > 0:
-            shifted = jnp.where((after >= offset)[:, None], shifted, jnp.zeros_like(shifted))
-        pieces.append(shifted)
-    stacked = jnp.concatenate(pieces, axis=1)
-    flat_weight = conv_weight.reshape(tap_count * conv_weight.shape[1], feat_width)
-    pre_act = jnp.dot(stacked, flat_weight, preferred_element_type=jnp.float32) + conv_bias
-    features = jax.nn.gelu(pre_act, approximate=False).astype(jnp.bfloat16)
-    joined = jnp.concatenate([features, labels[0].astype(jnp.bfloat16)], axis=1)
-    moments = lax.dot_general(
-        features, joined, (((0,), (0,)), ((), ())), preferred_element_type=jnp.float32
-    )
-    totals = jnp.sum(joined, axis=0, dtype=jnp.float32)
-
-    row_blocks = feat_width // BLOCK
-    col_blocks = row_blocks + label_width // BLOCK
+    frames = inputs.shape[1]
+    feats = conv_weight.shape[2]
+    row_blocks = feats // BLOCK
+    col_blocks = row_blocks + labels.shape[2] // BLOCK
     kept = [(i, j) for i in range(row_blocks) for j in range(i, col_blocks)]
-    blocks = [
-        moments[i * BLOCK : (i + 1) * BLOCK, j * BLOCK : (j + 1) * BLOCK] for i, j in kept
-    ]
-    total_rows = totals.reshape(-1, BLOCK)
-    blocks.append(jnp.pad(total_rows, ((0, BLOCK - total_rows.shape[0]), (0, 0))))
-    if len(blocks) % 2:
-        blocks.append(jnp.zeros((BLOCK, BLOCK), jnp.float32))
-    payload = jnp.concatenate(blocks, axis=0).reshape(2, -1, BLOCK)
-    mine, other = all_sum(payload)
-    frame_count = lax.axis_size(("x", "z", "y", "core")) * inputs.shape[0] * shard_rows
+    core = lax.axis_index("core").astype(jnp.int32)[None]
+    ahead, behind = frame_halo(inputs[0], TAP_REACH)
+    features, keep, send = front(
+        core,
+        inputs[0],
+        ahead,
+        behind,
+        conv_weight.reshape(-1, feats),
+        conv_bias[None],
+        labels[0],
+        rec_span[:, 0].reshape(2, -1, BLOCK),
+        kept,
+    )
+    mine, other = all_sum(keep, send)
+    frame_count = lax.axis_size(("x", "z", "y", "core")) * inputs.shape[0] * frames
     probe_weights = ridge_solve(mine, other, kept, row_blocks, col_blocks, frame_count)
     return (features[None], probe_weights)
 

time: 118 us -> 108 us (0.915)
  matrix products: 8.84 us -> 0 us
  Pallas kernels: 23.8 us -> 31.3 us
  other arithmetic: 7.65 us -> 1.32 us
  local copies, waits for them, and re-layouts: 6.43 us -> 1.36 us
  waiting for transfers between devices: 11.8 us -> 13.4 us
  starting transfers between devices: 17.6 us -> 18.9 us
    dot_general x2 -> x0, matrix products: 8.84 us -> none  [the longest x1 7.55 us: per_device(): jnp.dot(stacked, flat_weight, preferred_element_type=jnp.float32)]
    pallas_call x0 -> x1, Pallas kernels: none -> 8.27 us  [front(): pl.pallas_call(functools.partial(front_kernel, kept), out_shape=[jax.Shap...]
    unnamed x29 -> x4, local copies, waits for them, and re-layouts: 5.47 us -> 0.58 us
    convert_element_type x1 -> x0, other arithmetic: 2.82 us -> none  [per_device(): joined = jnp.concatenate([features, labels[0].astype(jnp.bfloat16)], axis=1)]
    ppermute x1, starting transfers between devices: 1.05 us -> 3.45 us  [all_sum(): part = keep + lax.ppermute(send, 'core', swap)]
    unnamed x3 -> x0, other arithmetic: 2.34 us -> none
    ppermute x1, waiting for transfers between devices: 0.01 us -> 2.01 us  [all_sum(): other = lax.ppermute(mine, 'core', swap)]
    all_to_all x1, blocking collectives: 25.2 us -> 26.7 us  [all_sum(): lax.all_to_all(part.reshape(peers, rows, BLOCK), ('x', 'y'), split_axis=0...]
  transfers between devices with their start and end apart: 7 -> 8, of which waited for: 4 -> 6; matrix products, arithmetic and copies ran while one was open for 9% -> 0% of each run, Pallas kernels for 0% -> 0%
where the time goes in v2:
time: 108 us
  blocking collectives  41 us (38%)
  Pallas kernels  31.3 us (29%)
  starting transfers between devices  18.9 us (17%)
  waiting for transfers between devices  13.4 us (12%)
  local copies, waits for them, and re-layouts  1.36 us (1%)
  other arithmetic  1.32 us (1%)
    all_to_all x1, blocking collectives, all_sum(): lax.all_to_all(part.reshape(peers, rows, BLOCK), ('x', 'y'), split_axis=0...  26.7 us
    pallas_call x1, Pallas kernels, ridge_solve(): pl.pallas_call(functools.partial(solve_kernel, kept, row_blocks, col_bloc...  23 us
    all_to_all x1, blocking collectives, all_sum(): lax.all_to_all(spread, ('x', 'y'), split_axis=0, concat_axis=0, tiled=True)  14.3 us
    ppermute x4, waiting for transfers between devices, all_sum(): lax.ppermute(chunk, 'z', [(i, i ^ bit) for i in range(lax.axis_size('z'))])  8.53 us
    pallas_call x1, Pallas kernels, front(): pl.pallas_call(functools.partial(front_kernel, kept), out_shape=[jax.Shap...  8.27 us
    ppermute x1, starting transfers between devices, all_sum(): other = lax.ppermute(mine, 'core', swap)  5.17 us
    ppermute x1, starting transfers between devices, frame_halo(): before = lax.ppermute(rows[-width:], ('x', 'z'), up)  5 us
    ppermute x4, starting transfers between devices, all_sum(): lax.ppermute(chunk, 'z', [(i, i ^ bit) for i in range(lax.axis_size('z'))])  3.97 us
  transfers between devices with their start and end apart: 8, of which 6 were waited for; matrix products, arithmetic and copies ran while one was open for 0% of the time, Pallas kernels for 0%

profile of v2, /device:TPU:1, one launch (start us, length us, event | category | flops | bytes accessed | tf_op | source)
XLA Modules:
  0.0 108.0 jit_solution(8942875829883613518)
XLA Ops:
  0.6 0.7 slice_bitcast_fusion
  1.4 1.3 %collective-permute-start.1 = (bf16[2,512]{1,0:T(2,128)(2,1)S(1)}, bf16[2,512]{1,0:T(2,128)(2,1)S(1)}, u32[]{:S(2)}, u32[]{:S(2)}) collective-permute-start(bf16[2,512]{1,0:T(2,128)(2,1)S(1)} %get-tuple-element.8), channel_id=1, source_target_pairs={{8,0},{16,8},{24,16},{32,24},{40,32},{48,40},{56,48},{64,56},{72,6... | collective-permute-start | bytes 6152 | tf_op jit(solution)/shard_map/ppermute | solution.py:26
  2.6 5.0 %collective-permute-start = (bf16[2,512]{1,0:T(2,128)(2,1)S(1)}, bf16[2,512]{1,0:T(2,128)(2,1)S(1)}, u32[]{:S(2)}, u32[]{:S(2)}) collective-permute-start(bf16[2,512]{1,0:T(2,128)(2,1)S(1)} %get-tuple-element.9), channel_id=1, source_target_pairs={{0,8},{8,16},{16,24},{24,32},{32,40},{40,48},{48,56},{56,64},{64,7... | collective-permute-start | bytes 6152 | tf_op jit(solution)/shard_map/ppermute | solution.py:25
  7.7 0.0 collective-permute-done.1.behind_hbm
  7.7 0.0 copy-start
  7.7 0.7 collective-permute-done.ahead_hbm
  8.4 0.0 copy-start.1
  8.4 0.0 copy-done
  8.4 0.6 copy-done.1
  8.9 8.3 %front.1 = (bf16[1024,512]{1,0:T(8,128)(2,1)}, f32[1664,128]{1,0:T(8,128)}, f32[1664,128]{1,0:T(8,128)}) custom-call(s32[1]{0:T(128)} %bitcast.core_ref, bf16[1024,512]{1,0:T(8,128)(2,1)} %bitcast.18, bf16[2,512]{1,0:T(2,128)(2,1)} %copy-done.1, bf16[2,512]{1,0:T(2,128)(2,1)} %copy-done, bf16[2560,512]{1,0:T(8,128)(2,1)} %bitcast.16, f32[1,512]{1,0:T(1,128)} %bitcast.20, ...), custom_call_target="tpu_custom_call" | custom-call | tf_op jit(solution)/shard_map/front/pallas_call | solution.py:168
  17.2 3.4 %collective-permute-start.2 = (f32[1664,128]{1,0:T(8,128)}, f32[1664,128]{1,0:T(8,128)S(1)}, u32[]{:S(2)}, u32[]{:S(2)}) collective-permute-start(f32[1664,128]{1,0:T(8,128)} %get-tuple-element.7), channel_id=1, source_target_pairs={{0,1},{1,0},{2,3},{3,2},{4,5},{5,4},{6,7},{7,6},{8,9},{9,8},{10,11... | collective-permute-start | bytes 2555912 | tf_op jit(solution)/shard_map/ppermute | solution.py:32
  20.7 2.2 %collective-permute-done.2 = f32[1664,128]{1,0:T(8,128)S(1)} collective-permute-done((f32[1664,128]{1,0:T(8,128)}, f32[1664,128]{1,0:T(8,128)S(1)}, u32[]{:S(2)}, u32[]{:S(2)}) %collective-permute-start.2) | collective-permute-done | bytes 852000 | tf_op jit(solution)/shard_map/ppermute | solution.py:32
  22.9 1.2 %add.15 = f32[1664,128]{1,0:T(8,128)S(1)} add(f32[1664,128]{1,0:T(8,128)} %get-tuple-element.6, f32[1664,128]{1,0:T(8,128)S(1)} %collective-permute-done.2) | non-fusion elementwise | flops 212992 | bytes 2555904 | tf_op jit(solution)/shard_map/add | solution.py:32
  24.1 26.7 %all_to_all.10 = f32[16,104,128]{2,1,0:T(8,128)S(1)} all-to-all(f32[16,104,128]{2,1,0:T(8,128)S(1)} %bitcast.15), channel_id=1, replica_groups=mesh['x'=4,'z'=8,'y'=4,'core'=2] {'x','y'}, dimensions={0} | all-to-all | bytes 1703936 | tf_op jit(solution)/shard_map/all_to_all | solution.py:35
  50.9 0.4 collective-permute-start.3
  51.3 6.6 %collective-permute-done.3 = f32[104,128]{1,0:T(8,128)S(1)} collective-permute-done((f32[104,128]{1,0:T(8,128)S(1)}, f32[104,128]{1,0:T(8,128)S(1)}, u32[]{:S(2)}, u32[]{:S(2)}) %collective-permute-start.3) | collective-permute-done | bytes 53280 | tf_op jit(solution)/shard_map/ppermute | solution.py:41
  57.9 0.1 collective-permute-start.6
  58.0 0.1 collective-permute-start.5
  58.1 3.4 %collective-permute-start.4 = (f32[104,128]{1,0:T(8,128)S(1)}, f32[104,128]{1,0:T(8,128)S(1)}, u32[]{:S(2)}, u32[]{:S(2)}) collective-permute-start(f32[104,128]{1,0:T(8,128)S(1)} %add.16), channel_id=1, source_target_pairs={{0,8},{8,0},{16,24},{24,16},{32,40},{40,32},{48,56},{56,48},{1,9},... | collective-permute-start | bytes 159752 | tf_op jit(solution)/shard_map/ppermute | solution.py:41
  61.5 1.4 %collective-permute-done.6 = f32[104,128]{1,0:T(8,128)S(1)} collective-permute-done((f32[104,128]{1,0:T(8,128)S(1)}, f32[104,128]{1,0:T(8,128)S(1)}, u32[]{:S(2)}, u32[]{:S(2)}) %collective-permute-start.6) | collective-permute-done | bytes 53280 | tf_op jit(solution)/shard_map/ppermute | solution.py:41
  62.9 0.0 collective-permute-done.5
  62.9 0.5 collective-permute-done.4
  63.5 0.1 broadcast_in_dim.19
  63.5 14.3 %all_to_all.11 = f32[16,104,128]{2,1,0:T(8,128)S(1)} all-to-all(f32[16,104,128]{2,1,0:T(8,128)S(1)} %broadcast_in_dim.19), channel_id=1, replica_groups=mesh['x'=4,'z'=8,'y'=4,'core'=2] {'x','y'}, dimensions={0} | all-to-all | bytes 1703936 | tf_op jit(solution)/shard_map/all_to_all | solution.py:45
  77.8 5.2 %collective-permute-start.7 = (f32[1664,128]{1,0:T(8,128)S(1)}, f32[1664,128]{1,0:T(8,128)S(1)}, u32[]{:S(2)}, u32[]{:S(2)}) collective-permute-start(f32[1664,128]{1,0:T(8,128)S(1)} %bitcast.13), channel_id=1, source_target_pairs={{0,1},{1,0},{2,3},{3,2},{4,5},{5,4},{6,7},{7,6},{8,9},{9,8},{10,11... | collective-permute-start | bytes 2555912 | tf_op jit(solution)/shard_map/ppermute | solution.py:47
  83.0 2.0 %collective-permute-done.7.other_ref = f32[1664,128]{1,0:T(8,128)S(1)} collective-permute-done((f32[1664,128]{1,0:T(8,128)S(1)}, f32[1664,128]{1,0:T(8,128)S(1)}, u32[]{:S(2)}, u32[]{:S(2)}) %collective-permute-start.7) | collective-permute-done | bytes 852000 | tf_op jit(solution)/shard_map/ppermute | solution.py:47
  85.0 23.0 %ridge_solve.1 = f32[512,512]{1,0:T(8,128)} custom-call(s32[1]{0:T(128)} %bitcast.core_ref, f32[1664,128]{1,0:T(8,128)S(1)} %bitcast.14, f32[1664,128]{1,0:T(8,128)S(1)} %collective-permute-done.7.other_ref), custom_call_target="tpu_custom_call" | custom-call | tf_op jit(solution)/shard_map/ridge_solve/pallas_call | solution.py:329
  (3 shorter events, 0.1 us)
Async XLA Ops:
  1.4 6.3 %collective-permute-start.1 = (bf16[2,512]{1,0:T(2,128)(2,1)S(1)}, bf16[2,512]{1,0:T(2,128)(2,1)S(1)}, u32[]{:S(2)}, u32[]{:S(2)}) collective-permute-start(bf16[2,512]{1,0:T(2,128)(2,1)S(1)} %get-tuple-element.8), channel_id=1, source_target_pairs={{8,0},{16,8},{24,16},{32,24},{40,32},{48,40},{56,48},{64,56},{72,6... | collective-permute-start | bytes 6152 | tf_op jit(solution)/shard_map/ppermute | solution.py:26
  2.6 5.7 %collective-permute-start = (bf16[2,512]{1,0:T(2,128)(2,1)S(1)}, bf16[2,512]{1,0:T(2,128)(2,1)S(1)}, u32[]{:S(2)}, u32[]{:S(2)}) collective-permute-start(bf16[2,512]{1,0:T(2,128)(2,1)S(1)} %get-tuple-element.9), channel_id=1, source_target_pairs={{0,8},{8,16},{16,24},{24,32},{32,40},{40,48},{48,56},{56,64},{64,7... | collective-permute-start | bytes 6152 | tf_op jit(solution)/shard_map/ppermute | solution.py:25
  7.7 0.7 copy-start
  8.4 0.6 copy-start.1
  17.2 5.7 %collective-permute-start.2 = (f32[1664,128]{1,0:T(8,128)}, f32[1664,128]{1,0:T(8,128)S(1)}, u32[]{:S(2)}, u32[]{:S(2)}) collective-permute-start(f32[1664,128]{1,0:T(8,128)} %get-tuple-element.7), channel_id=1, source_target_pairs={{0,1},{1,0},{2,3},{3,2},{4,5},{5,4},{6,7},{7,6},{8,9},{9,8},{10,11... | collective-permute-start | bytes 2555912 | tf_op jit(solution)/shard_map/ppermute | solution.py:32
  50.9 7.0 %collective-permute-start.3 = (f32[104,128]{1,0:T(8,128)S(1)}, f32[104,128]{1,0:T(8,128)S(1)}, u32[]{:S(2)}, u32[]{:S(2)}) collective-permute-start(f32[104,128]{1,0:T(8,128)S(1)} %reduce_sum.9), channel_id=1, source_target_pairs={{0,32},{8,40},{16,48},{24,56},{32,0},{40,8},{48,16},{56,24},{1,33}... | collective-permute-start | bytes 159752 | tf_op jit(solution)/shard_map/ppermute | solution.py:41
  57.9 5.0 %collective-permute-start.6 = (f32[104,128]{1,0:T(8,128)S(1)}, f32[104,128]{1,0:T(8,128)S(1)}, u32[]{:S(2)}, u32[]{:S(2)}) collective-permute-start(f32[104,128]{1,0:T(8,128)S(1)} %add.16), channel_id=1, source_target_pairs={{0,24},{8,16},{16,8},{24,0},{32,56},{40,48},{48,40},{56,32},{1,25}... | collective-permute-start | bytes 159752 | tf_op jit(solution)/shard_map/ppermute | solution.py:41
  58.0 4.9 %collective-permute-start.5 = (f32[104,128]{1,0:T(8,128)S(1)}, f32[104,128]{1,0:T(8,128)S(1)}, u32[]{:S(2)}, u32[]{:S(2)}) collective-permute-start(f32[104,128]{1,0:T(8,128)S(1)} %add.16), channel_id=1, source_target_pairs={{0,16},{8,24},{16,0},{24,8},{32,48},{40,56},{48,32},{56,40},{1,17}... | collective-permute-start | bytes 159752 | tf_op jit(solution)/shard_map/ppermute | solution.py:41
  58.1 5.3 %collective-permute-start.4 = (f32[104,128]{1,0:T(8,128)S(1)}, f32[104,128]{1,0:T(8,128)S(1)}, u32[]{:S(2)}, u32[]{:S(2)}) collective-permute-start(f32[104,128]{1,0:T(8,128)S(1)} %add.16), channel_id=1, source_target_pairs={{0,8},{8,0},{16,24},{24,16},{32,40},{40,32},{48,56},{56,48},{1,9},... | collective-permute-start | bytes 159752 | tf_op jit(solution)/shard_map/ppermute | solution.py:41
  77.8 7.2 %collective-permute-start.7 = (f32[1664,128]{1,0:T(8,128)S(1)}, f32[1664,128]{1,0:T(8,128)S(1)}, u32[]{:S(2)}, u32[]{:S(2)}) collective-permute-start(f32[1664,128]{1,0:T(8,128)S(1)} %bitcast.13), channel_id=1, source_target_pairs={{0,1},{1,0},{2,3},{3,2},{4,5},{5,4},{6,7},{7,6},{8,9},{9,8},{10,11... | collective-permute-start | bytes 2555912 | tf_op jit(solution)/shard_map/ppermute | solution.py:47

commit v3 on v2

--- a/solution.py
+++ b/solution.py
@@ -11,6 +11,7 @@
 RIDGE = 0.1
 BLOCK = 128
 GROUP = 8
+STRIP = 3
 TAP_REACH = 2
 PAD = 8
 ROWS = 256
@@ -184,35 +185,26 @@
     )(core, *arrays)
 
 
-def group_inverse(diag, rows):
+def group_solve(diag, rows):
     size = len(rows)
-    for j in range(0, size, 2):
-        a, b, c = diag[j][j], diag[j][j + 1], diag[j + 1][j + 1]
-        scale = 1.0 / (a * c - b * b)
-        left = [diag[i][j] for i in range(size)]
-        right = [diag[i][j + 1] for i in range(size)]
-
-        def solved(upper, lower):
-            return (c * upper - b * lower) * scale, (a * lower - b * upper) * scale
-
-        new = {k: solved(diag[j][k], diag[j + 1][k]) for k in range(j + 2, size)}
-        for i in range(size):
-            if i in (j, j + 1):
-                continue
-            for k in range(max(j + 2, i) if i > j else j + 2, size):
-                diag[i][k] = diag[i][k] - left[i] * new[k][0] - right[i] * new[k][1]
-                if i > j:
-                    diag[k][i] = diag[i][k]
-        for k in range(j + 2, size):
-            diag[j][k], diag[j + 1][k] = new[k]
-        rows[j], rows[j + 1] = solved(rows[j], rows[j + 1])
-        for i in range(size):
-            if i not in (j, j + 1):
-                rows[i] = rows[i] - left[i] * rows[j] - right[i] * rows[j + 1]
+    scale = []
+    lower = [[None] * size for _ in range(size)]
+    for j in range(size):
+        scale.append(1.0 / diag[j][j])
+        for i in range(j + 1, size):
+            lower[i][j] = diag[j][i] * scale[j]
+        for i in range(j + 1, size):
+            for k in range(i, size):
+                diag[i][k] = diag[i][k] - lower[i][j] * diag[j][k]
+            rows[i] = rows[i] - lower[i][j] * rows[j]
+    rows = [row * s for row, s in zip(rows, scale)]
+    for j in reversed(range(size)):
+        for i in range(j):
+            rows[i] = rows[i] - lower[j][i] * rows[j]
     return rows
 
 
-def spd_inverse(block):
+def spd_inverse(block, spot, beside):
     groups = BLOCK // GROUP
     tile = (GROUP, BLOCK)
     lane = lax.broadcasted_iota(jnp.int32, tile, 1)
@@ -228,11 +220,12 @@
     def pivots(g):
         first = g * GROUP
         inside = (lane >= first) & (lane < first + GROUP)
-        cols = columns(g, first)
-        diag = [[None] * GROUP for _ in range(GROUP)]
-        for i in range(GROUP):
-            for j in range(i, GROUP):
-                diag[i][j] = diag[j][i] = spread(cols[i][j : j + 1])
+        for i, column in enumerate(columns(g, first)):
+            spot[g % 2, i] = column
+        diag = [
+            [spread(spot[g % 2, i, j : j + 1]) if j >= i else None for j in range(GROUP)]
+            for i in range(GROUP)
+        ]
         rows = [
             jnp.where(
                 lane == first + i, 1.0, jnp.where(inside, 0.0, spread(part[g][i : i + 1]))
@@ -246,7 +239,7 @@
         inside, diag, rows = ahead
         others = [(g + n) % groups for n in range(1, groups)]
         cols = {h: columns(h, g * GROUP) for h in others}
-        rows = group_inverse(diag, rows)
+        rows = group_solve(diag, rows)
 
         def eliminate(h):
             terms = [cols[h][j] * rows[j] for j in range(GROUP)]
@@ -257,6 +250,8 @@
         eliminate(others[0])
         if g + 1 < groups:
             ahead = pivots(g + 1)
+        for call in beside[g * len(beside) // groups : (g + 1) * len(beside) // groups]:
+            call()
         for h in others[1:]:
             eliminate(h)
         for i in range(GROUP):
@@ -268,7 +263,9 @@
     return jnp.dot(a, b, precision=lax.Precision.HIGHEST, preferred_element_type=jnp.float32)
 
 
-def solve_kernel(kept, row_blocks, col_blocks, frame_count, core_ref, mine_ref, other_ref, out_ref, work):
+def solve_kernel(
+    kept, row_blocks, col_blocks, frame_count, core_ref, mine_ref, other_ref, out_ref, work, flipped, inverse, spot
+):
     core = core_ref[0]
     half = mine_ref.shape[0] // BLOCK
 
@@ -280,64 +277,94 @@
     def span(i, j=None):
         return slice(i * BLOCK, (i + 1 if j is None else j) * BLOCK)
 
-    diagonal = lax.broadcasted_iota(jnp.int32, (BLOCK, BLOCK), 0) == lax.broadcasted_iota(
-        jnp.int32, (BLOCK, BLOCK), 1
-    )
+    row = lax.broadcasted_iota(jnp.int32, (BLOCK, BLOCK), 0)
+    column = lax.broadcasted_iota(jnp.int32, (BLOCK, BLOCK), 1)
     middle = BLOCK // 2
-    lane = lax.broadcasted_iota(jnp.int32, (1, BLOCK), 1)
-    wanted = (lax.broadcasted_iota(jnp.int32, (BLOCK, BLOCK), 0) < middle) | (
-        lax.broadcasted_iota(jnp.int32, (BLOCK, BLOCK), 1) >= middle
-    )
-    across = [None] * col_blocks
-    squares = []
-    for i in range(row_blocks):
-        square = summed(kept.index((i, i)))
-        riding = square[middle : middle + 8]
+    totals = {}
+
+    def read_totals(i):
+        riding = summed(kept.index((i, i)))[middle : middle + 8]
         for n, j in enumerate((i, i + row_blocks)):
-            total = jnp.where(
-                lane < middle,
+            totals[j] = jnp.where(
+                lax.broadcasted_iota(jnp.int32, (1, BLOCK), 1) < middle,
                 riding[2 * n : 2 * n + 1],
                 pltpu.roll(riding[2 * n + 1 : 2 * n + 2], middle, 1),
             )
-            across[j] = jnp.broadcast_to(total, (BLOCK, BLOCK))
-        squares.append(jnp.where(wanted, square, square.T))
-    down = [across[i].T for i in range(row_blocks)]
-    for n, (i, j) in enumerate(kept):
-        centred = (squares[i] if i == j else summed(n)) - down[i] * across[j] / frame_count
+
+    def across(j):
+        return jnp.broadcast_to(totals[j], (BLOCK, BLOCK))
+
+    downs = {}
+
+    def build(i, j):
+        block = summed(kept.index((i, j)))
+        if i == j:
+            block = jnp.where((row < middle) | (column >= middle), block, block.T)
+        if i not in downs:
+            downs[i] = across(i).T
+        centred = block - downs[i] * across(j) / frame_count
         if j >= row_blocks:
             work[span(i), span(j)] = centred / math.sqrt(frame_count)
         else:
             block = centred / frame_count
-            work[span(i), span(j)] = jnp.where(diagonal, block + RIDGE, block) if i == j else block
+            work[span(i), span(j)] = jnp.where(row == column, block + RIDGE, block) if i == j else block
+
+    def flip(k, i):
+        flipped[k % 2, span(i), :] = work[span(k), span(i)].T
+
+    for i in range(row_blocks):
+        read_totals(i)
+    build(0, 0)
+    beside = [functools.partial(build, i, j) for i, j in kept if j]
+    beside += [functools.partial(flip, 0, i) for i in range(1, row_blocks)]
+
+    def solve_row(k, at):
+        work[span(k), at] = dot32(inverse[k % 2], work[span(k), at])
+
+    def eliminate(i, k, at):
+        left = flipped[k % 2, span(i), :] if i > k else work[span(i), span(k)]
+        work[span(i), at] -= dot32(left, work[span(k), at])
+
+    def chunks(first):
+        cuts = list(range(col_blocks, first, -STRIP))[::-1]
+        return [span(max(first, cut - STRIP), cut) for cut in cuts]
 
     for k in range(row_blocks):
-        rest = span(k + 1, col_blocks)
-        inverse = spd_inverse(work[span(k), span(k)])
-        flipped = {i: work[span(k), span(i)].T for i in range(k + 1, row_blocks)}
-        solved = dot32(inverse, work[span(k), rest])
-        work[span(k), rest] = solved
-        for i in range(k + 1, row_blocks):
-            at = span(i, col_blocks)
-            work[span(i), at] -= dot32(flipped[i], solved[:, (i - k - 1) * BLOCK :])
-        if k:
-            work[span(0, k), rest] -= dot32(work[span(0, k), span(k)], solved)
+        inverse[k % 2] = spd_inverse(work[span(k), span(k)], spot, beside)
+        near = k + 1
+        beside = []
+        if near < row_blocks:
+            solve_row(k, span(near))
+            eliminate(near, k, span(near))
+        far = min(near + 1, col_blocks) if near < row_blocks else row_blocks
+        for at in chunks(far):
+            beside.append(functools.partial(solve_row, k, at))
+        for i in sorted((i for i in range(row_blocks) if i != k), key=lambda i: (i != near, i)):
+            first = near if i < k and near < row_blocks else max(i, far)
+            for at in chunks(first):
+                beside.append(functools.partial(eliminate, i, k, at))
+        beside += [functools.partial(flip, near, i) for i in range(near + 1, row_blocks)]
+    for call in beside:
+        call()
     out_ref[...] = work[:, span(row_blocks, col_blocks)]
 
 
 def ridge_solve(mine, other, kept, row_blocks, col_blocks, frame_count):
     core = lax.axis_index("core").astype(jnp.int32)[None]
+    vmem = pl.BlockSpec(memory_space=pltpu.VMEM)
     return pl.pallas_call(
         functools.partial(solve_kernel, kept, row_blocks, col_blocks, float(frame_count)),
         out_shape=jax.ShapeDtypeStruct(
             (row_blocks * BLOCK, (col_blocks - row_blocks) * BLOCK), jnp.float32
         ),
-        in_specs=[
-            pl.BlockSpec(memory_space=pltpu.SMEM),
-            pl.BlockSpec(memory_space=pltpu.VMEM),
-            pl.BlockSpec(memory_space=pltpu.VMEM),
+        in_specs=[pl.BlockSpec(memory_space=pltpu.SMEM), vmem, vmem],
+        out_specs=vmem,
+        scratch_shapes=[
+            pltpu.VMEM((row_blocks * BLOCK, col_blocks * BLOCK), jnp.float32),
+            pltpu.VMEM((2, row_blocks * BLOCK, BLOCK), jnp.float32),
+            pltpu.VMEM((2, BLOCK, BLOCK), jnp.float32),
+            pltpu.VMEM((2, GROUP, GROUP, BLOCK), jnp.float32),
         ],
-        out_specs=pl.BlockSpec(memory_space=pltpu.VMEM),
-        scratch_shapes=[pltpu.VMEM((row_blocks * BLOCK, col_blocks * BLOCK), jnp.float32)],
         compiler_params=pltpu.CompilerParams(vmem_limit_bytes=SOLVE_VMEM),
         name="ridge_solve",
     )(core, mine, other)

time: 108 us -> 105 us (0.972)
  Pallas kernels: 31.3 us -> 28.1 us
    pallas_call x1, Pallas kernels: 23 us -> 19.9 us  [ridge_solve(): pl.pallas_call(functools.partial(solve_kernel, kept, row_blocks, col_bloc...]
where the time goes in v3:
time: 105 us
  blocking collectives  41 us (39%)
  Pallas kernels  28.1 us (27%)
  starting transfers between devices  18.9 us (18%)
  waiting for transfers between devices  13.4 us (13%)
  local copies, waits for them, and re-layouts  1.36 us (1%)
  other arithmetic  1.32 us (1%)
    all_to_all x1, blocking collectives, all_sum(): lax.all_to_all(part.reshape(peers, rows, BLOCK), ('x', 'y'), split_axis=0...  26.7 us
    pallas_call x1, Pallas kernels, ridge_solve(): pl.pallas_call(functools.partial(solve_kernel, kept, row_blocks, col_bloc...  19.9 us
    all_to_all x1, blocking collectives, all_sum(): lax.all_to_all(spread, ('x', 'y'), split_axis=0, concat_axis=0, tiled=True)  14.3 us
    ppermute x4, waiting for transfers between devices, all_sum(): lax.ppermute(chunk, 'z', [(i, i ^ bit) for i in range(lax.axis_size('z'))])  8.53 us
    pallas_call x1, Pallas kernels, front(): pl.pallas_call(functools.partial(front_kernel, kept), out_shape=[jax.Shap...  8.27 us
    ppermute x1, starting transfers between devices, all_sum(): other = lax.ppermute(mine, 'core', swap)  5.17 us
    ppermute x1, starting transfers between devices, frame_halo(): before = lax.ppermute(rows[-width:], ('x', 'z'), up)  5 us
    ppermute x4, starting transfers between devices, all_sum(): lax.ppermute(chunk, 'z', [(i, i ^ bit) for i in range(lax.axis_size('z'))])  3.97 us
  transfers between devices with their start and end apart: 8, of which 6 were waited for; matrix products, arithmetic and copies ran while one was open for 0% of the time, Pallas kernels for 0%

profile of v3, /device:TPU:1, one launch (start us, length us, event | category | flops | bytes accessed | tf_op | source)
XLA Modules:
  0.0 104.9 jit_solution(2120454332619411309)
XLA Ops:
  0.6 0.7 slice_bitcast_fusion
  1.4 1.3 %collective-permute-start.1 = (bf16[2,512]{1,0:T(2,128)(2,1)S(1)}, bf16[2,512]{1,0:T(2,128)(2,1)S(1)}, u32[]{:S(2)}, u32[]{:S(2)}) collective-permute-start(bf16[2,512]{1,0:T(2,128)(2,1)S(1)} %get-tuple-element.8), channel_id=1, source_target_pairs={{8,0},{16,8},{24,16},{32,24},{40,32},{48,40},{56,48},{64,56},{72,6... | collective-permute-start | bytes 6152 | tf_op jit(solution)/shard_map/ppermute | solution.py:27
  2.6 5.0 %collective-permute-start = (bf16[2,512]{1,0:T(2,128)(2,1)S(1)}, bf16[2,512]{1,0:T(2,128)(2,1)S(1)}, u32[]{:S(2)}, u32[]{:S(2)}) collective-permute-start(bf16[2,512]{1,0:T(2,128)(2,1)S(1)} %get-tuple-element.9), channel_id=1, source_target_pairs={{0,8},{8,16},{16,24},{24,32},{32,40},{40,48},{48,56},{56,64},{64,7... | collective-permute-start | bytes 6152 | tf_op jit(solution)/shard_map/ppermute | solution.py:26
  7.7 0.0 collective-permute-done.1.behind_hbm
  7.7 0.0 copy-start
  7.7 0.7 collective-permute-done.ahead_hbm
  8.4 0.0 copy-start.1
  8.4 0.0 copy-done
  8.4 0.6 copy-done.1
  8.9 8.3 %front.1 = (bf16[1024,512]{1,0:T(8,128)(2,1)}, f32[1664,128]{1,0:T(8,128)}, f32[1664,128]{1,0:T(8,128)}) custom-call(s32[1]{0:T(128)} %bitcast.core_ref, bf16[1024,512]{1,0:T(8,128)(2,1)} %bitcast.18, bf16[2,512]{1,0:T(2,128)(2,1)} %copy-done.1, bf16[2,512]{1,0:T(2,128)(2,1)} %copy-done, bf16[2560,512]{1,0:T(8,128)(2,1)} %bitcast.16, f32[1,512]{1,0:T(1,128)} %bitcast.20, ...), custom_call_target="tpu_custom_call" | custom-call | tf_op jit(solution)/shard_map/front/pallas_call | solution.py:169
  17.2 3.4 %collective-permute-start.2 = (f32[1664,128]{1,0:T(8,128)}, f32[1664,128]{1,0:T(8,128)S(1)}, u32[]{:S(2)}, u32[]{:S(2)}) collective-permute-start(f32[1664,128]{1,0:T(8,128)} %get-tuple-element.7), channel_id=1, source_target_pairs={{0,1},{1,0},{2,3},{3,2},{4,5},{5,4},{6,7},{7,6},{8,9},{9,8},{10,11... | collective-permute-start | bytes 2555912 | tf_op jit(solution)/shard_map/ppermute | solution.py:33
  20.7 2.2 %collective-permute-done.2 = f32[1664,128]{1,0:T(8,128)S(1)} collective-permute-done((f32[1664,128]{1,0:T(8,128)}, f32[1664,128]{1,0:T(8,128)S(1)}, u32[]{:S(2)}, u32[]{:S(2)}) %collective-permute-start.2) | collective-permute-done | bytes 852000 | tf_op jit(solution)/shard_map/ppermute | solution.py:33
  22.9 1.2 %add.15 = f32[1664,128]{1,0:T(8,128)S(1)} add(f32[1664,128]{1,0:T(8,128)} %get-tuple-element.6, f32[1664,128]{1,0:T(8,128)S(1)} %collective-permute-done.2) | non-fusion elementwise | flops 212992 | bytes 2555904 | tf_op jit(solution)/shard_map/add | solution.py:33
  24.1 26.7 %all_to_all.10 = f32[16,104,128]{2,1,0:T(8,128)S(1)} all-to-all(f32[16,104,128]{2,1,0:T(8,128)S(1)} %bitcast.15), channel_id=1, replica_groups=mesh['x'=4,'z'=8,'y'=4,'core'=2] {'x','y'}, dimensions={0} | all-to-all | bytes 1703936 | tf_op jit(solution)/shard_map/all_to_all | solution.py:36
  50.9 0.4 collective-permute-start.3
  51.3 6.6 %collective-permute-done.3 = f32[104,128]{1,0:T(8,128)S(1)} collective-permute-done((f32[104,128]{1,0:T(8,128)S(1)}, f32[104,128]{1,0:T(8,128)S(1)}, u32[]{:S(2)}, u32[]{:S(2)}) %collective-permute-start.3) | collective-permute-done | bytes 53280 | tf_op jit(solution)/shard_map/ppermute | solution.py:42
  57.9 0.1 collective-permute-start.6
  58.0 0.1 collective-permute-start.5
  58.1 3.4 %collective-permute-start.4 = (f32[104,128]{1,0:T(8,128)S(1)}, f32[104,128]{1,0:T(8,128)S(1)}, u32[]{:S(2)}, u32[]{:S(2)}) collective-permute-start(f32[104,128]{1,0:T(8,128)S(1)} %add.16), channel_id=1, source_target_pairs={{0,8},{8,0},{16,24},{24,16},{32,40},{40,32},{48,56},{56,48},{1,9},... | collective-permute-start | bytes 159752 | tf_op jit(solution)/shard_map/ppermute | solution.py:42
  61.5 1.4 %collective-permute-done.6 = f32[104,128]{1,0:T(8,128)S(1)} collective-permute-done((f32[104,128]{1,0:T(8,128)S(1)}, f32[104,128]{1,0:T(8,128)S(1)}, u32[]{:S(2)}, u32[]{:S(2)}) %collective-permute-start.6) | collective-permute-done | bytes 53280 | tf_op jit(solution)/shard_map/ppermute | solution.py:42
  62.9 0.0 collective-permute-done.5
  62.9 0.5 collective-permute-done.4
  63.5 0.1 broadcast_in_dim.19
  63.5 14.3 %all_to_all.11 = f32[16,104,128]{2,1,0:T(8,128)S(1)} all-to-all(f32[16,104,128]{2,1,0:T(8,128)S(1)} %broadcast_in_dim.19), channel_id=1, replica_groups=mesh['x'=4,'z'=8,'y'=4,'core'=2] {'x','y'}, dimensions={0} | all-to-all | bytes 1703936 | tf_op jit(solution)/shard_map/all_to_all | solution.py:46
  77.8 5.2 %collective-permute-start.7 = (f32[1664,128]{1,0:T(8,128)S(1)}, f32[1664,128]{1,0:T(8,128)S(1)}, u32[]{:S(2)}, u32[]{:S(2)}) collective-permute-start(f32[1664,128]{1,0:T(8,128)S(1)} %bitcast.13), channel_id=1, source_target_pairs={{0,1},{1,0},{2,3},{3,2},{4,5},{5,4},{6,7},{7,6},{8,9},{9,8},{10,11... | collective-permute-start | bytes 2555912 | tf_op jit(solution)/shard_map/ppermute | solution.py:48
  83.0 2.0 %collective-permute-done.7.other_ref = f32[1664,128]{1,0:T(8,128)S(1)} collective-permute-done((f32[1664,128]{1,0:T(8,128)S(1)}, f32[1664,128]{1,0:T(8,128)S(1)}, u32[]{:S(2)}, u32[]{:S(2)}) %collective-permute-start.7) | collective-permute-done | bytes 852000 | tf_op jit(solution)/shard_map/ppermute | solution.py:48
  85.0 19.9 %ridge_solve.1 = f32[512,512]{1,0:T(8,128)} custom-call(s32[1]{0:T(128)} %bitcast.core_ref, f32[1664,128]{1,0:T(8,128)S(1)} %bitcast.14, f32[1664,128]{1,0:T(8,128)S(1)} %collective-permute-done.7.other_ref), custom_call_target="tpu_custom_call" | custom-call | tf_op jit(solution)/shard_map/ridge_solve/pallas_call | solution.py:355
  (3 shorter events, 0.1 us)
Async XLA Ops:
  1.4 6.3 %collective-permute-start.1 = (bf16[2,512]{1,0:T(2,128)(2,1)S(1)}, bf16[2,512]{1,0:T(2,128)(2,1)S(1)}, u32[]{:S(2)}, u32[]{:S(2)}) collective-permute-start(bf16[2,512]{1,0:T(2,128)(2,1)S(1)} %get-tuple-element.8), channel_id=1, source_target_pairs={{8,0},{16,8},{24,16},{32,24},{40,32},{48,40},{56,48},{64,56},{72,6... | collective-permute-start | bytes 6152 | tf_op jit(solution)/shard_map/ppermute | solution.py:27
  2.6 5.7 %collective-permute-start = (bf16[2,512]{1,0:T(2,128)(2,1)S(1)}, bf16[2,512]{1,0:T(2,128)(2,1)S(1)}, u32[]{:S(2)}, u32[]{:S(2)}) collective-permute-start(bf16[2,512]{1,0:T(2,128)(2,1)S(1)} %get-tuple-element.9), channel_id=1, source_target_pairs={{0,8},{8,16},{16,24},{24,32},{32,40},{40,48},{48,56},{56,64},{64,7... | collective-permute-start | bytes 6152 | tf_op jit(solution)/shard_map/ppermute | solution.py:26
  7.7 0.7 copy-start
  8.4 0.6 copy-start.1
  17.2 5.7 %collective-permute-start.2 = (f32[1664,128]{1,0:T(8,128)}, f32[1664,128]{1,0:T(8,128)S(1)}, u32[]{:S(2)}, u32[]{:S(2)}) collective-permute-start(f32[1664,128]{1,0:T(8,128)} %get-tuple-element.7), channel_id=1, source_target_pairs={{0,1},{1,0},{2,3},{3,2},{4,5},{5,4},{6,7},{7,6},{8,9},{9,8},{10,11... | collective-permute-start | bytes 2555912 | tf_op jit(solution)/shard_map/ppermute | solution.py:33
  50.9 7.0 %collective-permute-start.3 = (f32[104,128]{1,0:T(8,128)S(1)}, f32[104,128]{1,0:T(8,128)S(1)}, u32[]{:S(2)}, u32[]{:S(2)}) collective-permute-start(f32[104,128]{1,0:T(8,128)S(1)} %reduce_sum.9), channel_id=1, source_target_pairs={{0,32},{8,40},{16,48},{24,56},{32,0},{40,8},{48,16},{56,24},{1,33}... | collective-permute-start | bytes 159752 | tf_op jit(solution)/shard_map/ppermute | solution.py:42
  57.9 5.0 %collective-permute-start.6 = (f32[104,128]{1,0:T(8,128)S(1)}, f32[104,128]{1,0:T(8,128)S(1)}, u32[]{:S(2)}, u32[]{:S(2)}) collective-permute-start(f32[104,128]{1,0:T(8,128)S(1)} %add.16), channel_id=1, source_target_pairs={{0,24},{8,16},{16,8},{24,0},{32,56},{40,48},{48,40},{56,32},{1,25}... | collective-permute-start | bytes 159752 | tf_op jit(solution)/shard_map/ppermute | solution.py:42
  58.0 4.9 %collective-permute-start.5 = (f32[104,128]{1,0:T(8,128)S(1)}, f32[104,128]{1,0:T(8,128)S(1)}, u32[]{:S(2)}, u32[]{:S(2)}) collective-permute-start(f32[104,128]{1,0:T(8,128)S(1)} %add.16), channel_id=1, source_target_pairs={{0,16},{8,24},{16,0},{24,8},{32,48},{40,56},{48,32},{56,40},{1,17}... | collective-permute-start | bytes 159752 | tf_op jit(solution)/shard_map/ppermute | solution.py:42
  58.1 5.3 %collective-permute-start.4 = (f32[104,128]{1,0:T(8,128)S(1)}, f32[104,128]{1,0:T(8,128)S(1)}, u32[]{:S(2)}, u32[]{:S(2)}) collective-permute-start(f32[104,128]{1,0:T(8,128)S(1)} %add.16), channel_id=1, source_target_pairs={{0,8},{8,0},{16,24},{24,16},{32,40},{40,32},{48,56},{56,48},{1,9},... | collective-permute-start | bytes 159752 | tf_op jit(solution)/shard_map/ppermute | solution.py:42
  77.8 7.2 %collective-permute-start.7 = (f32[1664,128]{1,0:T(8,128)S(1)}, f32[1664,128]{1,0:T(8,128)S(1)}, u32[]{:S(2)}, u32[]{:S(2)}) collective-permute-start(f32[1664,128]{1,0:T(8,128)S(1)} %bitcast.13), channel_id=1, source_target_pairs={{0,1},{1,0},{2,3},{3,2},{4,5},{5,4},{6,7},{7,6},{8,9},{9,8},{10,11... | collective-permute-start | bytes 2555912 | tf_op jit(solution)/shard_map/ppermute | solution.py:48

commit v4 on v3

--- a/solution.py
+++ b/solution.py
@@ -15,7 +15,7 @@
 TAP_REACH = 2
 PAD = 8
 ROWS = 256
-FRONT_VMEM = 60 * 1024 * 1024
+FRONT_VMEM = 28 * 1024 * 1024
 SOLVE_VMEM = 16 * 1024 * 1024
 
 
@@ -67,15 +67,17 @@
     loads = [
         pltpu.make_async_copy(source, target, sems.at[n])
         for n, (source, target) in enumerate(
-            (
-                (inputs_hbm, inputs),
+            [
                 (ahead_hbm, ahead),
                 (behind_hbm, behind),
                 (span_hbm, span),
                 (bias_hbm, bias),
-                (weight_hbm, weight),
-                (labels_hbm, labels),
-            )
+            ]
+            + [
+                (inputs_hbm.at[first : first + ROWS], inputs.at[first : first + ROWS])
+                for first in range(0, frames, ROWS)
+            ]
+            + [(weight_hbm, weight), (labels_hbm, labels)]
         )
     ]
     for load in loads:
@@ -85,9 +87,15 @@
     gap = jnp.zeros((PAD - TAP_REACH, width), jnp.float32)
     wide[0:PAD, :] = jnp.concatenate([gap, ahead[...].astype(jnp.float32)], axis=0)
     wide[PAD + frames :, :] = jnp.concatenate([behind[...].astype(jnp.float32), gap], axis=0)
-    wide[PAD : PAD + frames, :] = inputs[...].astype(jnp.float32)
+    ready = 0
     for start in range(0, frames, BLOCK):
         at = slice(start, start + BLOCK)
+        need = min((start + BLOCK) // ROWS + 1, frames // ROWS)
+        for n in range(ready, need):
+            loads[4 + n].wait()
+            arrived = slice(n * ROWS, (n + 1) * ROWS)
+            wide[PAD + n * ROWS : PAD + (n + 1) * ROWS, :] = inputs[arrived, :].astype(jnp.float32)
+        ready = need
         line = slice(start // BLOCK, start // BLOCK + 1)
         spans = [
             jnp.concatenate([down_lanes(span[side, line, :].astype(jnp.float32))] * (width // BLOCK), axis=1)
@@ -101,8 +109,7 @@
                 shifted = wide[PAD + start + offset : PAD + start + offset + BLOCK, :]
                 inside = spans[int(offset > 0)] >= abs(offset) - 0.5
                 taps[at, columns] = jnp.where(inside, shifted, 0.0).astype(jnp.bfloat16)
-    for load in loads[4:6]:
-        load.wait()
+    loads[-2].wait()
     stores = []
     for tile, first in enumerate(range(0, frames, ROWS)):
         rows = slice(first, first + ROWS)
@@ -114,7 +121,7 @@
             pltpu.make_async_copy(features.at[rows], features_hbm.at[rows], sems.at[len(loads) + tile])
         )
         stores[-1].start()
-    loads[6].wait()
+    loads[-1].wait()
     joined[:, feats:] = labels[...].astype(jnp.float32).astype(jnp.bfloat16)
 
     totals = jnp.dot(
@@ -163,6 +170,10 @@
     frames, width = rows.shape
     feats = weight.shape[1]
     taps = weight.shape[0]
+    rows, weight, bias, labels, span = (
+        pltpu.with_memory_space_constraint(array, pltpu.HBM)
+        for array in (rows, weight, bias, labels, span)
+    )
     arrays = (rows, ahead, behind, weight, bias, labels, span)
     hbm = pl.BlockSpec(memory_space=pltpu.HBM)
     half = jax.ShapeDtypeStruct((len(kept) // 2 * BLOCK, BLOCK), jnp.float32)
@@ -178,14 +189,20 @@
             pltpu.VMEM((frames, feats + labels.shape[1]), jnp.bfloat16),
             pltpu.VMEM((frames, feats), jnp.bfloat16),
             pltpu.VMEM((2,) + half.shape, jnp.float32),
-            pltpu.SemaphoreType.DMA((len(arrays) + frames // ROWS + 2,)),
+            pltpu.SemaphoreType.DMA((len(arrays) - 1 + 2 * (frames // ROWS) + 2,)),
         ],
         compiler_params=pltpu.CompilerParams(vmem_limit_bytes=FRONT_VMEM),
         name="front",
     )(core, *arrays)
 
 
-def group_solve(diag, rows):
+def tree_sum(terms):
+    while len(terms) > 1:
+        terms = [terms[n] + terms[n + 1] for n in range(0, len(terms), 2)]
+    return terms[0]
+
+
+def group_solve(diag, rows, near):
     size = len(rows)
     scale = []
     lower = [[None] * size for _ in range(size)]
@@ -201,7 +218,7 @@
     for j in reversed(range(size)):
         for i in range(j):
             rows[i] = rows[i] - lower[j][i] * rows[j]
-    return rows
+    return rows, tree_sum([column * row for column, row in zip(near, rows)])
 
 
 def spd_inverse(block, spot, beside):
@@ -239,21 +256,15 @@
         inside, diag, rows = ahead
         others = [(g + n) % groups for n in range(1, groups)]
         cols = {h: columns(h, g * GROUP) for h in others}
-        rows = group_solve(diag, rows)
-
-        def eliminate(h):
-            terms = [cols[h][j] * rows[j] for j in range(GROUP)]
-            while len(terms) > 1:
-                terms = [terms[n] + terms[n + 1] for n in range(0, len(terms), 2)]
-            part[h] = jnp.where(inside, 0.0, part[h]) - terms[0]
-
-        eliminate(others[0])
+        rows, product = group_solve(diag, rows, cols[others[0]])
+        part[others[0]] = jnp.where(inside, 0.0, part[others[0]]) - product
         if g + 1 < groups:
             ahead = pivots(g + 1)
         for call in beside[g * len(beside) // groups : (g + 1) * len(beside) // groups]:
             call()
         for h in others[1:]:
-            eliminate(h)
+            product = tree_sum([column * row for column, row in zip(cols[h], rows)])
+            part[h] = jnp.where(inside, 0.0, part[h]) - product
         for i in range(GROUP):
             part[g] = jnp.where(sublane == i, rows[i], part[g])
     return jnp.concatenate(part, axis=0)
@@ -264,7 +275,7 @@
 
 
 def solve_kernel(
-    kept, row_blocks, col_blocks, frame_count, core_ref, mine_ref, other_ref, out_ref, work, flipped, inverse, spot
+    kept, row_blocks, col_blocks, frame_count, core_ref, mine_ref, other_ref, out_hbm, work, flipped, inverse, spot, sems
 ):
     core = core_ref[0]
     half = mine_ref.shape[0] // BLOCK
@@ -332,21 +343,32 @@
     for k in range(row_blocks):
         inverse[k % 2] = spd_inverse(work[span(k), span(k)], spot, beside)
         near = k + 1
+        if near == row_blocks:
+            break
+        solve_row(k, span(near))
+        eliminate(near, k, span(near))
+        far = near + 1
         beside = []
-        if near < row_blocks:
-            solve_row(k, span(near))
-            eliminate(near, k, span(near))
-        far = min(near + 1, col_blocks) if near < row_blocks else row_blocks
         for at in chunks(far):
             beside.append(functools.partial(solve_row, k, at))
         for i in sorted((i for i in range(row_blocks) if i != k), key=lambda i: (i != near, i)):
-            first = near if i < k and near < row_blocks else max(i, far)
+            first = near if i < k else max(i, far)
             for at in chunks(first):
                 beside.append(functools.partial(eliminate, i, k, at))
         beside += [functools.partial(flip, near, i) for i in range(near + 1, row_blocks)]
-    for call in beside:
-        call()
-    out_ref[...] = work[:, span(row_blocks, col_blocks)]
+    last = row_blocks - 1
+    answer = span(row_blocks, col_blocks)
+    solve_row(last, answer)
+    copies = []
+    for i in (last, *range(last)):
+        if i != last:
+            eliminate(i, last, answer)
+        copies.append(
+            pltpu.make_async_copy(work.at[span(i), answer], out_hbm.at[span(i)], sems.at[i])
+        )
+        copies[-1].start()
+    for copy in copies:
+        copy.wait()
 
 
 def ridge_solve(mine, other, kept, row_blocks, col_blocks, frame_count):
@@ -358,12 +380,13 @@
             (row_blocks * BLOCK, (col_blocks - row_blocks) * BLOCK), jnp.float32
         ),
         in_specs=[pl.BlockSpec(memory_space=pltpu.SMEM), vmem, vmem],
-        out_specs=vmem,
+        out_specs=pl.BlockSpec(memory_space=pltpu.HBM),
         scratch_shapes=[
             pltpu.VMEM((row_blocks * BLOCK, col_blocks * BLOCK), jnp.float32),
             pltpu.VMEM((2, row_blocks * BLOCK, BLOCK), jnp.float32),
             pltpu.VMEM((2, BLOCK, BLOCK), jnp.float32),
             pltpu.VMEM((2, GROUP, GROUP, BLOCK), jnp.float32),
+            pltpu.SemaphoreType.DMA((row_blocks,)),
         ],
         compiler_params=pltpu.CompilerParams(vmem_limit_bytes=SOLVE_VMEM),
         name="ridge_solve",

time: 105 us -> 102 us (0.971)
  other arithmetic: 1.32 us -> 0.2 us
    add x1, other arithmetic: 1.24 us -> 0.12 us  [all_sum(): part = keep + lax.ppermute(send, 'core', swap)]
where the time goes in v4:
time: 102 us
  blocking collectives  41 us (40%)
  Pallas kernels  27.1 us (27%)
  starting transfers between devices  18.9 us (19%)
  waiting for transfers between devices  13.3 us (13%)
    all_to_all x1, blocking collectives, all_sum(): lax.all_to_all(part.reshape(peers, rows, BLOCK), ('x', 'y'), split_axis=0...  26.7 us
    pallas_call x1, Pallas kernels, ridge_solve(): pl.pallas_call(functools.partial(solve_kernel, kept, row_blocks, col_bloc...  19.7 us
    all_to_all x1, blocking collectives, all_sum(): lax.all_to_all(spread, ('x', 'y'), split_axis=0, concat_axis=0, tiled=True)  14.3 us
    ppermute x4, waiting for transfers between devices, all_sum(): lax.ppermute(chunk, 'z', [(i, i ^ bit) for i in range(lax.axis_size('z'))])  8.53 us
    pallas_call x1, Pallas kernels, front(): pl.pallas_call(functools.partial(front_kernel, kept), out_shape=[jax.Shap...  7.34 us
    ppermute x1, starting transfers between devices, all_sum(): other = lax.ppermute(mine, 'core', swap)  5.17 us
    ppermute x1, starting transfers between devices, frame_halo(): before = lax.ppermute(rows[-width:], ('x', 'z'), up)  5 us
    ppermute x4, starting transfers between devices, all_sum(): lax.ppermute(chunk, 'z', [(i, i ^ bit) for i in range(lax.axis_size('z'))])  3.97 us
  transfers between devices with their start and end apart: 8, of which 6 were waited for; matrix products, arithmetic and copies ran while one was open for 0% of the time, Pallas kernels for 0%

profile of v4, /device:TPU:1, one launch (start us, length us, event | category | flops | bytes accessed | tf_op | source)
XLA Modules:
  0.0 102.1 jit_solution(2857652425392058322)
XLA Ops:
  0.6 0.7 slice_bitcast_fusion
  1.4 1.3 %collective-permute-start.1 = (bf16[2,512]{1,0:T(2,128)(2,1)S(1)}, bf16[2,512]{1,0:T(2,128)(2,1)S(1)}, u32[]{:S(2)}, u32[]{:S(2)}) collective-permute-start(bf16[2,512]{1,0:T(2,128)(2,1)S(1)} %get-tuple-element.8), channel_id=1, source_target_pairs={{8,0},{16,8},{24,16},{32,24},{40,32},{48,40},{56,48},{64,56},{72,6... | collective-permute-start | bytes 6152 | tf_op jit(solution)/shard_map/ppermute | solution.py:27
  2.6 5.0 %collective-permute-start = (bf16[2,512]{1,0:T(2,128)(2,1)S(1)}, bf16[2,512]{1,0:T(2,128)(2,1)S(1)}, u32[]{:S(2)}, u32[]{:S(2)}) collective-permute-start(bf16[2,512]{1,0:T(2,128)(2,1)S(1)} %get-tuple-element.9), channel_id=1, source_target_pairs={{0,8},{8,16},{16,24},{24,32},{32,40},{40,48},{48,56},{56,64},{64,7... | collective-permute-start | bytes 6152 | tf_op jit(solution)/shard_map/ppermute | solution.py:26
  7.7 0.0 collective-permute-done.1.behind_hbm
  7.7 0.7 collective-permute-done.ahead_hbm
  8.4 7.3 %front.1 = (bf16[1024,512]{1,0:T(8,128)(2,1)}, f32[1664,128]{1,0:T(8,128)S(1)}, f32[1664,128]{1,0:T(8,128)S(1)}) custom-call(s32[1]{0:T(128)} %bitcast.core_ref, bf16[1024,512]{1,0:T(8,128)(2,1)} %bitcast.18, bf16[2,512]{1,0:T(2,128)(2,1)S(1)} %collective-permute-done.ahead_hbm, bf16[2,512]{1,0:T(2,128)(2,1)S(1)} %collective-permute-done.1.behind_hbm, ...), custom_call_target="tpu_custom_call" | custom-call | tf_op jit(solution)/shard_map/front/pallas_call | solution.py:180
  15.7 3.5 %collective-permute-start.2 = (f32[1664,128]{1,0:T(8,128)S(1)}, f32[1664,128]{1,0:T(8,128)S(1)}, u32[]{:S(2)}, u32[]{:S(2)}) collective-permute-start(f32[1664,128]{1,0:T(8,128)S(1)} %get-tuple-element.7), channel_id=1, source_target_pairs={{0,1},{1,0},{2,3},{3,2},{4,5},{5,4},{6,7},{7,6},{8,9},{9,8},{10,11... | collective-permute-start | bytes 2555912 | tf_op jit(solution)/shard_map/ppermute | solution.py:33
  19.2 2.0 %collective-permute-done.2 = f32[1664,128]{1,0:T(8,128)S(1)} collective-permute-done((f32[1664,128]{1,0:T(8,128)S(1)}, f32[1664,128]{1,0:T(8,128)S(1)}, u32[]{:S(2)}, u32[]{:S(2)}) %collective-permute-start.2) | collective-permute-done | bytes 852000 | tf_op jit(solution)/shard_map/ppermute | solution.py:33
  21.2 0.1 add.15
  21.3 26.7 %all_to_all.10 = f32[16,104,128]{2,1,0:T(8,128)S(1)} all-to-all(f32[16,104,128]{2,1,0:T(8,128)S(1)} %bitcast.15), channel_id=1, replica_groups=mesh['x'=4,'z'=8,'y'=4,'core'=2] {'x','y'}, dimensions={0} | all-to-all | bytes 1703936 | tf_op jit(solution)/shard_map/all_to_all | solution.py:36
  48.1 0.3 collective-permute-start.3
  48.4 6.6 %collective-permute-done.3 = f32[104,128]{1,0:T(8,128)S(1)} collective-permute-done((f32[104,128]{1,0:T(8,128)S(1)}, f32[104,128]{1,0:T(8,128)S(1)}, u32[]{:S(2)}, u32[]{:S(2)}) %collective-permute-start.3) | collective-permute-done | bytes 53280 | tf_op jit(solution)/shard_map/ppermute | solution.py:42
  55.1 0.1 collective-permute-start.6
  55.2 0.1 collective-permute-start.5
  55.3 3.4 %collective-permute-start.4 = (f32[104,128]{1,0:T(8,128)S(1)}, f32[104,128]{1,0:T(8,128)S(1)}, u32[]{:S(2)}, u32[]{:S(2)}) collective-permute-start(f32[104,128]{1,0:T(8,128)S(1)} %add.16), channel_id=1, source_target_pairs={{0,8},{8,0},{16,24},{24,16},{32,40},{40,32},{48,56},{56,48},{1,9},... | collective-permute-start | bytes 159752 | tf_op jit(solution)/shard_map/ppermute | solution.py:42
  58.7 1.4 %collective-permute-done.6 = f32[104,128]{1,0:T(8,128)S(1)} collective-permute-done((f32[104,128]{1,0:T(8,128)S(1)}, f32[104,128]{1,0:T(8,128)S(1)}, u32[]{:S(2)}, u32[]{:S(2)}) %collective-permute-start.6) | collective-permute-done | bytes 53280 | tf_op jit(solution)/shard_map/ppermute | solution.py:42
  60.1 0.0 collective-permute-done.5
  60.1 0.5 collective-permute-done.4
  60.6 0.1 broadcast_in_dim.19
  60.7 14.3 %all_to_all.11 = f32[16,104,128]{2,1,0:T(8,128)S(1)} all-to-all(f32[16,104,128]{2,1,0:T(8,128)S(1)} %broadcast_in_dim.19), channel_id=1, replica_groups=mesh['x'=4,'z'=8,'y'=4,'core'=2] {'x','y'}, dimensions={0} | all-to-all | bytes 1703936 | tf_op jit(solution)/shard_map/all_to_all | solution.py:46
  75.0 5.2 %collective-permute-start.7 = (f32[1664,128]{1,0:T(8,128)S(1)}, f32[1664,128]{1,0:T(8,128)S(1)}, u32[]{:S(2)}, u32[]{:S(2)}) collective-permute-start(f32[1664,128]{1,0:T(8,128)S(1)} %bitcast.13), channel_id=1, source_target_pairs={{0,1},{1,0},{2,3},{3,2},{4,5},{5,4},{6,7},{7,6},{8,9},{9,8},{10,11... | collective-permute-start | bytes 2555912 | tf_op jit(solution)/shard_map/ppermute | solution.py:48
  80.2 2.0 %collective-permute-done.7.other_ref = f32[1664,128]{1,0:T(8,128)S(1)} collective-permute-done((f32[1664,128]{1,0:T(8,128)S(1)}, f32[1664,128]{1,0:T(8,128)S(1)}, u32[]{:S(2)}, u32[]{:S(2)}) %collective-permute-start.7) | collective-permute-done | bytes 852000 | tf_op jit(solution)/shard_map/ppermute | solution.py:48
  82.2 19.7 %ridge_solve.1 = f32[512,512]{1,0:T(8,128)} custom-call(s32[1]{0:T(128)} %bitcast.core_ref, f32[1664,128]{1,0:T(8,128)S(1)} %bitcast.14, f32[1664,128]{1,0:T(8,128)S(1)} %collective-permute-done.7.other_ref), custom_call_target="tpu_custom_call" | custom-call | tf_op jit(solution)/shard_map/ridge_solve/pallas_call | solution.py:377
  (3 shorter events, 0.1 us)
Async XLA Ops:
  1.4 6.3 %collective-permute-start.1 = (bf16[2,512]{1,0:T(2,128)(2,1)S(1)}, bf16[2,512]{1,0:T(2,128)(2,1)S(1)}, u32[]{:S(2)}, u32[]{:S(2)}) collective-permute-start(bf16[2,512]{1,0:T(2,128)(2,1)S(1)} %get-tuple-element.8), channel_id=1, source_target_pairs={{8,0},{16,8},{24,16},{32,24},{40,32},{48,40},{56,48},{64,56},{72,6... | collective-permute-start | bytes 6152 | tf_op jit(solution)/shard_map/ppermute | solution.py:27
  2.6 5.7 %collective-permute-start = (bf16[2,512]{1,0:T(2,128)(2,1)S(1)}, bf16[2,512]{1,0:T(2,128)(2,1)S(1)}, u32[]{:S(2)}, u32[]{:S(2)}) collective-permute-start(bf16[2,512]{1,0:T(2,128)(2,1)S(1)} %get-tuple-element.9), channel_id=1, source_target_pairs={{0,8},{8,16},{16,24},{24,32},{32,40},{40,48},{48,56},{56,64},{64,7... | collective-permute-start | bytes 6152 | tf_op jit(solution)/shard_map/ppermute | solution.py:26
  15.7 5.5 %collective-permute-start.2 = (f32[1664,128]{1,0:T(8,128)S(1)}, f32[1664,128]{1,0:T(8,128)S(1)}, u32[]{:S(2)}, u32[]{:S(2)}) collective-permute-start(f32[1664,128]{1,0:T(8,128)S(1)} %get-tuple-element.7), channel_id=1, source_target_pairs={{0,1},{1,0},{2,3},{3,2},{4,5},{5,4},{6,7},{7,6},{8,9},{9,8},{10,11... | collective-permute-start | bytes 2555912 | tf_op jit(solution)/shard_map/ppermute | solution.py:33
  48.1 7.0 %collective-permute-start.3 = (f32[104,128]{1,0:T(8,128)S(1)}, f32[104,128]{1,0:T(8,128)S(1)}, u32[]{:S(2)}, u32[]{:S(2)}) collective-permute-start(f32[104,128]{1,0:T(8,128)S(1)} %reduce_sum.9), channel_id=1, source_target_pairs={{0,32},{8,40},{16,48},{24,56},{32,0},{40,8},{48,16},{56,24},{1,33}... | collective-permute-start | bytes 159752 | tf_op jit(solution)/shard_map/ppermute | solution.py:42
  55.1 5.0 %collective-permute-start.6 = (f32[104,128]{1,0:T(8,128)S(1)}, f32[104,128]{1,0:T(8,128)S(1)}, u32[]{:S(2)}, u32[]{:S(2)}) collective-permute-start(f32[104,128]{1,0:T(8,128)S(1)} %add.16), channel_id=1, source_target_pairs={{0,24},{8,16},{16,8},{24,0},{32,56},{40,48},{48,40},{56,32},{1,25}... | collective-permute-start | bytes 159752 | tf_op jit(solution)/shard_map/ppermute | solution.py:42
  55.2 4.9 %collective-permute-start.5 = (f32[104,128]{1,0:T(8,128)S(1)}, f32[104,128]{1,0:T(8,128)S(1)}, u32[]{:S(2)}, u32[]{:S(2)}) collective-permute-start(f32[104,128]{1,0:T(8,128)S(1)} %add.16), channel_id=1, source_target_pairs={{0,16},{8,24},{16,0},{24,8},{32,48},{40,56},{48,32},{56,40},{1,17}... | collective-permute-start | bytes 159752 | tf_op jit(solution)/shard_map/ppermute | solution.py:42
  55.3 5.3 %collective-permute-start.4 = (f32[104,128]{1,0:T(8,128)S(1)}, f32[104,128]{1,0:T(8,128)S(1)}, u32[]{:S(2)}, u32[]{:S(2)}) collective-permute-start(f32[104,128]{1,0:T(8,128)S(1)} %add.16), channel_id=1, source_target_pairs={{0,8},{8,0},{16,24},{24,16},{32,40},{40,32},{48,56},{56,48},{1,9},... | collective-permute-start | bytes 159752 | tf_op jit(solution)/shard_map/ppermute | solution.py:42
  75.0 7.2 %collective-permute-start.7 = (f32[1664,128]{1,0:T(8,128)S(1)}, f32[1664,128]{1,0:T(8,128)S(1)}, u32[]{:S(2)}, u32[]{:S(2)}) collective-permute-start(f32[1664,128]{1,0:T(8,128)S(1)} %bitcast.13), channel_id=1, source_target_pairs={{0,1},{1,0},{2,3},{3,2},{4,5},{5,4},{6,7},{7,6},{8,9},{9,8},{10,11... | collective-permute-start | bytes 2555912 | tf_op jit(solution)/shard_map/ppermute | solution.py:48

commit v5 on v4

--- a/solution.py
+++ b/solution.py
@@ -11,6 +11,7 @@
 RIDGE = 0.1
 BLOCK = 128
 GROUP = 8
+PANEL = 4
 STRIP = 3
 TAP_REACH = 2
 PAD = 8
@@ -202,7 +203,7 @@
     return terms[0]
 
 
-def group_solve(diag, rows, near):
+def group_solve(diag, rows):
     size = len(rows)
     scale = []
     lower = [[None] * size for _ in range(size)]
@@ -218,7 +219,7 @@
     for j in reversed(range(size)):
         for i in range(j):
             rows[i] = rows[i] - lower[j][i] * rows[j]
-    return rows, tree_sum([column * row for column, row in zip(near, rows)])
+    return rows
 
 
 def spd_inverse(block, spot, beside):
@@ -254,19 +255,40 @@
     ahead = pivots(0)
     for g in range(groups):
         inside, diag, rows = ahead
-        others = [(g + n) % groups for n in range(1, groups)]
-        cols = {h: columns(h, g * GROUP) for h in others}
-        rows, product = group_solve(diag, rows, cols[others[0]])
-        part[others[0]] = jnp.where(inside, 0.0, part[others[0]]) - product
+        panel = g // PANEL
+        final = (panel + 1) * PANEL >= groups
+        stepped = [
+            h for h in ((g + n) % groups for n in range(1, groups)) if final or 0 <= h // PANEL - panel <= 1
+        ]
+        cols = {h: columns(h, g * GROUP) for h in stepped}
+        rows = group_solve(diag, rows)
+
+        def eliminate(h):
+            product = tree_sum([column * row for column, row in zip(cols[h], rows)])
+            part[h] = jnp.where(inside, 0.0, part[h]) - product
+
         if g + 1 < groups:
+            eliminate(stepped[0])
             ahead = pivots(g + 1)
+            stepped = stepped[1:]
         for call in beside[g * len(beside) // groups : (g + 1) * len(beside) // groups]:
             call()
-        for h in others[1:]:
-            product = tree_sum([column * row for column, row in zip(cols[h], rows)])
-            part[h] = jnp.where(inside, 0.0, part[h]) - product
+        for h in stepped:
+            eliminate(h)
         for i in range(GROUP):
             part[g] = jnp.where(sublane == i, rows[i], part[g])
+        if not final and (g + 1) % PANEL == 0:
+            far = [h for h in range(groups) if not 0 <= h // PANEL - panel <= 1]
+            first = panel * PANEL * GROUP
+            inside = (lane >= first) & (lane < first + PANEL * GROUP)
+            factor = jnp.concatenate([jnp.where(inside, part[h], 0.0) for h in far], axis=0)
+            panel_rows = jnp.concatenate(
+                [part[h] if h // PANEL == panel else jnp.zeros(tile, jnp.float32) for h in range(groups)],
+                axis=0,
+            )
+            product = dot32(factor, panel_rows)
+            for n, h in enumerate(far):
+                part[h] = jnp.where(inside, 0.0, part[h]) - product[n * GROUP : (n + 1) * GROUP]
     return jnp.concatenate(part, axis=0)
 
 

time: 102 us -> 101 us (level)
  Pallas kernels: 27.1 us -> 25.4 us
    pallas_call x1, Pallas kernels: 19.7 us -> 18.1 us  [ridge_solve(): pl.pallas_call(functools.partial(solve_kernel, kept, row_blocks, col_bloc...]
where the time goes in v5:
time: 101 us; the launch traced here: 100 us
  blocking collectives  41 us (41%)
  Pallas kernels  25.4 us (25%)
  starting transfers between devices  18.9 us (19%)
  waiting for transfers between devices  13.3 us (13%)
    all_to_all x1, blocking collectives, all_sum(): lax.all_to_all(part.reshape(peers, rows, BLOCK), ('x', 'y'), split_axis=0...  26.7 us
    pallas_call x1, Pallas kernels, ridge_solve(): pl.pallas_call(functools.partial(solve_kernel, kept, row_blocks, col_bloc...  18.1 us
    all_to_all x1, blocking collectives, all_sum(): lax.all_to_all(spread, ('x', 'y'), split_axis=0, concat_axis=0, tiled=True)  14.3 us
    ppermute x4, waiting for transfers between devices, all_sum(): lax.ppermute(chunk, 'z', [(i, i ^ bit) for i in range(lax.axis_size('z'))])  8.53 us
    pallas_call x1, Pallas kernels, front(): pl.pallas_call(functools.partial(front_kernel, kept), out_shape=[jax.Shap...  7.34 us
    ppermute x1, starting transfers between devices, all_sum(): other = lax.ppermute(mine, 'core', swap)  5.17 us
    ppermute x1, starting transfers between devices, frame_halo(): before = lax.ppermute(rows[-width:], ('x', 'z'), up)  5 us
    ppermute x4, starting transfers between devices, all_sum(): lax.ppermute(chunk, 'z', [(i, i ^ bit) for i in range(lax.axis_size('z'))])  3.97 us
  transfers between devices with their start and end apart: 8, of which 6 were waited for; matrix products, arithmetic and copies ran while one was open for 0% of the time, Pallas kernels for 0%

profile of v5, /device:TPU:1, one launch (start us, length us, event | category | flops | bytes accessed | tf_op | source)
XLA Modules:
  0.0 100.4 jit_solution(11197090701835733651)
XLA Ops:
  0.6 0.7 slice_bitcast_fusion
  1.4 1.3 %collective-permute-start.1 = (bf16[2,512]{1,0:T(2,128)(2,1)S(1)}, bf16[2,512]{1,0:T(2,128)(2,1)S(1)}, u32[]{:S(2)}, u32[]{:S(2)}) collective-permute-start(bf16[2,512]{1,0:T(2,128)(2,1)S(1)} %get-tuple-element.8), channel_id=1, source_target_pairs={{8,0},{16,8},{24,16},{32,24},{40,32},{48,40},{56,48},{64,56},{72,6... | collective-permute-start | bytes 6152 | tf_op jit(solution)/shard_map/ppermute | solution.py:28
  2.6 5.0 %collective-permute-start = (bf16[2,512]{1,0:T(2,128)(2,1)S(1)}, bf16[2,512]{1,0:T(2,128)(2,1)S(1)}, u32[]{:S(2)}, u32[]{:S(2)}) collective-permute-start(bf16[2,512]{1,0:T(2,128)(2,1)S(1)} %get-tuple-element.9), channel_id=1, source_target_pairs={{0,8},{8,16},{16,24},{24,32},{32,40},{40,48},{48,56},{56,64},{64,7... | collective-permute-start | bytes 6152 | tf_op jit(solution)/shard_map/ppermute | solution.py:27
  7.7 0.0 collective-permute-done.1.behind_hbm
  7.7 0.7 collective-permute-done.ahead_hbm
  8.4 7.3 %front.1 = (bf16[1024,512]{1,0:T(8,128)(2,1)}, f32[1664,128]{1,0:T(8,128)S(1)}, f32[1664,128]{1,0:T(8,128)S(1)}) custom-call(s32[1]{0:T(128)} %bitcast.core_ref, bf16[1024,512]{1,0:T(8,128)(2,1)} %bitcast.18, bf16[2,512]{1,0:T(2,128)(2,1)S(1)} %collective-permute-done.ahead_hbm, bf16[2,512]{1,0:T(2,128)(2,1)S(1)} %collective-permute-done.1.behind_hbm, ...), custom_call_target="tpu_custom_call" | custom-call | tf_op jit(solution)/shard_map/front/pallas_call | solution.py:181
  15.7 3.5 %collective-permute-start.2 = (f32[1664,128]{1,0:T(8,128)S(1)}, f32[1664,128]{1,0:T(8,128)S(1)}, u32[]{:S(2)}, u32[]{:S(2)}) collective-permute-start(f32[1664,128]{1,0:T(8,128)S(1)} %get-tuple-element.7), channel_id=1, source_target_pairs={{0,1},{1,0},{2,3},{3,2},{4,5},{5,4},{6,7},{7,6},{8,9},{9,8},{10,11... | collective-permute-start | bytes 2555912 | tf_op jit(solution)/shard_map/ppermute | solution.py:34
  19.2 2.0 %collective-permute-done.2 = f32[1664,128]{1,0:T(8,128)S(1)} collective-permute-done((f32[1664,128]{1,0:T(8,128)S(1)}, f32[1664,128]{1,0:T(8,128)S(1)}, u32[]{:S(2)}, u32[]{:S(2)}) %collective-permute-start.2) | collective-permute-done | bytes 852000 | tf_op jit(solution)/shard_map/ppermute | solution.py:34
  21.2 0.1 add.15
  21.3 26.7 %all_to_all.10 = f32[16,104,128]{2,1,0:T(8,128)S(1)} all-to-all(f32[16,104,128]{2,1,0:T(8,128)S(1)} %bitcast.15), channel_id=1, replica_groups=mesh['x'=4,'z'=8,'y'=4,'core'=2] {'x','y'}, dimensions={0} | all-to-all | bytes 1703936 | tf_op jit(solution)/shard_map/all_to_all | solution.py:37
  48.1 0.3 collective-permute-start.3
  48.4 6.6 %collective-permute-done.3 = f32[104,128]{1,0:T(8,128)S(1)} collective-permute-done((f32[104,128]{1,0:T(8,128)S(1)}, f32[104,128]{1,0:T(8,128)S(1)}, u32[]{:S(2)}, u32[]{:S(2)}) %collective-permute-start.3) | collective-permute-done | bytes 53280 | tf_op jit(solution)/shard_map/ppermute | solution.py:43
  55.1 0.1 collective-permute-start.6
  55.2 0.1 collective-permute-start.5
  55.3 3.4 %collective-permute-start.4 = (f32[104,128]{1,0:T(8,128)S(1)}, f32[104,128]{1,0:T(8,128)S(1)}, u32[]{:S(2)}, u32[]{:S(2)}) collective-permute-start(f32[104,128]{1,0:T(8,128)S(1)} %add.16), channel_id=1, source_target_pairs={{0,8},{8,0},{16,24},{24,16},{32,40},{40,32},{48,56},{56,48},{1,9},... | collective-permute-start | bytes 159752 | tf_op jit(solution)/shard_map/ppermute | solution.py:43
  58.7 1.4 %collective-permute-done.6 = f32[104,128]{1,0:T(8,128)S(1)} collective-permute-done((f32[104,128]{1,0:T(8,128)S(1)}, f32[104,128]{1,0:T(8,128)S(1)}, u32[]{:S(2)}, u32[]{:S(2)}) %collective-permute-start.6) | collective-permute-done | bytes 53280 | tf_op jit(solution)/shard_map/ppermute | solution.py:43
  60.1 0.0 collective-permute-done.5
  60.1 0.5 collective-permute-done.4
  60.6 0.1 broadcast_in_dim.19
  60.7 14.3 %all_to_all.11 = f32[16,104,128]{2,1,0:T(8,128)S(1)} all-to-all(f32[16,104,128]{2,1,0:T(8,128)S(1)} %broadcast_in_dim.19), channel_id=1, replica_groups=mesh['x'=4,'z'=8,'y'=4,'core'=2] {'x','y'}, dimensions={0} | all-to-all | bytes 1703936 | tf_op jit(solution)/shard_map/all_to_all | solution.py:47
  75.0 5.2 %collective-permute-start.7 = (f32[1664,128]{1,0:T(8,128)S(1)}, f32[1664,128]{1,0:T(8,128)S(1)}, u32[]{:S(2)}, u32[]{:S(2)}) collective-permute-start(f32[1664,128]{1,0:T(8,128)S(1)} %bitcast.13), channel_id=1, source_target_pairs={{0,1},{1,0},{2,3},{3,2},{4,5},{5,4},{6,7},{7,6},{8,9},{9,8},{10,11... | collective-permute-start | bytes 2555912 | tf_op jit(solution)/shard_map/ppermute | solution.py:49
  80.2 2.0 %collective-permute-done.7.other_ref = f32[1664,128]{1,0:T(8,128)S(1)} collective-permute-done((f32[1664,128]{1,0:T(8,128)S(1)}, f32[1664,128]{1,0:T(8,128)S(1)}, u32[]{:S(2)}, u32[]{:S(2)}) %collective-permute-start.7) | collective-permute-done | bytes 852000 | tf_op jit(solution)/shard_map/ppermute | solution.py:49
  82.2 18.1 %ridge_solve.1 = f32[512,512]{1,0:T(8,128)} custom-call(s32[1]{0:T(128)} %bitcast.core_ref, f32[1664,128]{1,0:T(8,128)S(1)} %bitcast.14, f32[1664,128]{1,0:T(8,128)S(1)} %collective-permute-done.7.other_ref), custom_call_target="tpu_custom_call" | custom-call | tf_op jit(solution)/shard_map/ridge_solve/pallas_call | solution.py:399
  (3 shorter events, 0.1 us)
Async XLA Ops:
  1.4 6.3 %collective-permute-start.1 = (bf16[2,512]{1,0:T(2,128)(2,1)S(1)}, bf16[2,512]{1,0:T(2,128)(2,1)S(1)}, u32[]{:S(2)}, u32[]{:S(2)}) collective-permute-start(bf16[2,512]{1,0:T(2,128)(2,1)S(1)} %get-tuple-element.8), channel_id=1, source_target_pairs={{8,0},{16,8},{24,16},{32,24},{40,32},{48,40},{56,48},{64,56},{72,6... | collective-permute-start | bytes 6152 | tf_op jit(solution)/shard_map/ppermute | solution.py:28
  2.6 5.7 %collective-permute-start = (bf16[2,512]{1,0:T(2,128)(2,1)S(1)}, bf16[2,512]{1,0:T(2,128)(2,1)S(1)}, u32[]{:S(2)}, u32[]{:S(2)}) collective-permute-start(bf16[2,512]{1,0:T(2,128)(2,1)S(1)} %get-tuple-element.9), channel_id=1, source_target_pairs={{0,8},{8,16},{16,24},{24,32},{32,40},{40,48},{48,56},{56,64},{64,7... | collective-permute-start | bytes 6152 | tf_op jit(solution)/shard_map/ppermute | solution.py:27
  15.7 5.5 %collective-permute-start.2 = (f32[1664,128]{1,0:T(8,128)S(1)}, f32[1664,128]{1,0:T(8,128)S(1)}, u32[]{:S(2)}, u32[]{:S(2)}) collective-permute-start(f32[1664,128]{1,0:T(8,128)S(1)} %get-tuple-element.7), channel_id=1, source_target_pairs={{0,1},{1,0},{2,3},{3,2},{4,5},{5,4},{6,7},{7,6},{8,9},{9,8},{10,11... | collective-permute-start | bytes 2555912 | tf_op jit(solution)/shard_map/ppermute | solution.py:34
  48.1 7.0 %collective-permute-start.3 = (f32[104,128]{1,0:T(8,128)S(1)}, f32[104,128]{1,0:T(8,128)S(1)}, u32[]{:S(2)}, u32[]{:S(2)}) collective-permute-start(f32[104,128]{1,0:T(8,128)S(1)} %reduce_sum.9), channel_id=1, source_target_pairs={{0,32},{8,40},{16,48},{24,56},{32,0},{40,8},{48,16},{56,24},{1,33}... | collective-permute-start | bytes 159752 | tf_op jit(solution)/shard_map/ppermute | solution.py:43
  55.1 5.0 %collective-permute-start.6 = (f32[104,128]{1,0:T(8,128)S(1)}, f32[104,128]{1,0:T(8,128)S(1)}, u32[]{:S(2)}, u32[]{:S(2)}) collective-permute-start(f32[104,128]{1,0:T(8,128)S(1)} %add.16), channel_id=1, source_target_pairs={{0,24},{8,16},{16,8},{24,0},{32,56},{40,48},{48,40},{56,32},{1,25}... | collective-permute-start | bytes 159752 | tf_op jit(solution)/shard_map/ppermute | solution.py:43
  55.2 4.9 %collective-permute-start.5 = (f32[104,128]{1,0:T(8,128)S(1)}, f32[104,128]{1,0:T(8,128)S(1)}, u32[]{:S(2)}, u32[]{:S(2)}) collective-permute-start(f32[104,128]{1,0:T(8,128)S(1)} %add.16), channel_id=1, source_target_pairs={{0,16},{8,24},{16,0},{24,8},{32,48},{40,56},{48,32},{56,40},{1,17}... | collective-permute-start | bytes 159752 | tf_op jit(solution)/shard_map/ppermute | solution.py:43
  55.3 5.3 %collective-permute-start.4 = (f32[104,128]{1,0:T(8,128)S(1)}, f32[104,128]{1,0:T(8,128)S(1)}, u32[]{:S(2)}, u32[]{:S(2)}) collective-permute-start(f32[104,128]{1,0:T(8,128)S(1)} %add.16), channel_id=1, source_target_pairs={{0,8},{8,0},{16,24},{24,16},{32,40},{40,32},{48,56},{56,48},{1,9},... | collective-permute-start | bytes 159752 | tf_op jit(solution)/shard_map/ppermute | solution.py:43
  75.0 7.2 %collective-permute-start.7 = (f32[1664,128]{1,0:T(8,128)S(1)}, f32[1664,128]{1,0:T(8,128)S(1)}, u32[]{:S(2)}, u32[]{:S(2)}) collective-permute-start(f32[1664,128]{1,0:T(8,128)S(1)} %bitcast.13), channel_id=1, source_target_pairs={{0,1},{1,0},{2,3},{3,2},{4,5},{5,4},{6,7},{7,6},{8,9},{9,8},{10,11... | collective-permute-start | bytes 2555912 | tf_op jit(solution)/shard_map/ppermute | solution.py:49

commit v6 on v5

--- a/solution.py
+++ b/solution.py
@@ -203,7 +203,8 @@
     return terms[0]
 
 
-def group_solve(diag, rows):
+def group_solve(diag, rows, near):
+    near = list(near)
     size = len(rows)
     scale = []
     lower = [[None] * size for _ in range(size)]
@@ -215,11 +216,13 @@
             for k in range(i, size):
                 diag[i][k] = diag[i][k] - lower[i][j] * diag[j][k]
             rows[i] = rows[i] - lower[i][j] * rows[j]
+            near[i] = near[i] - lower[i][j] * near[j]
     rows = [row * s for row, s in zip(rows, scale)]
+    product = tree_sum([column * row for column, row in zip(near, rows)])
     for j in reversed(range(size)):
         for i in range(j):
             rows[i] = rows[i] - lower[j][i] * rows[j]
-    return rows
+    return rows, product
 
 
 def spd_inverse(block, spot, beside):
@@ -261,14 +264,14 @@
             h for h in ((g + n) % groups for n in range(1, groups)) if final or 0 <= h // PANEL - panel <= 1
         ]
         cols = {h: columns(h, g * GROUP) for h in stepped}
-        rows = group_solve(diag, rows)
+        rows, product = group_solve(diag, rows, cols[stepped[0]])
 
         def eliminate(h):
             product = tree_sum([column * row for column, row in zip(cols[h], rows)])
             part[h] = jnp.where(inside, 0.0, part[h]) - product
 
         if g + 1 < groups:
-            eliminate(stepped[0])
+            part[stepped[0]] = jnp.where(inside, 0.0, part[stepped[0]]) - product
             ahead = pivots(g + 1)
             stepped = stepped[1:]
         for call in beside[g * len(beside) // groups : (g + 1) * len(beside) // groups]:

time: 101 us -> 99.3 us (0.983)
  Pallas kernels: 25.4 us -> 23.9 us
    pallas_call x1, Pallas kernels: 18.1 us -> 16.5 us  [ridge_solve(): pl.pallas_call(functools.partial(solve_kernel, kept, row_blocks, col_bloc...]
where the time goes in v6:
time: 99.3 us; the launch traced here: 98.9 us
  blocking collectives  41 us (41%)
  Pallas kernels  23.9 us (24%)
  starting transfers between devices  18.9 us (19%)
  waiting for transfers between devices  13.3 us (13%)
    all_to_all x1, blocking collectives, all_sum(): lax.all_to_all(part.reshape(peers, rows, BLOCK), ('x', 'y'), split_axis=0...  26.7 us
    pallas_call x1, Pallas kernels, ridge_solve(): pl.pallas_call(functools.partial(solve_kernel, kept, row_blocks, col_bloc...  16.5 us
    all_to_all x1, blocking collectives, all_sum(): lax.all_to_all(spread, ('x', 'y'), split_axis=0, concat_axis=0, tiled=True)  14.3 us
    ppermute x4, waiting for transfers between devices, all_sum(): lax.ppermute(chunk, 'z', [(i, i ^ bit) for i in range(lax.axis_size('z'))])  8.53 us
    pallas_call x1, Pallas kernels, front(): pl.pallas_call(functools.partial(front_kernel, kept), out_shape=[jax.Shap...  7.34 us
    ppermute x1, starting transfers between devices, all_sum(): other = lax.ppermute(mine, 'core', swap)  5.17 us
    ppermute x1, starting transfers between devices, frame_halo(): before = lax.ppermute(rows[-width:], ('x', 'z'), up)  5 us
    ppermute x4, starting transfers between devices, all_sum(): lax.ppermute(chunk, 'z', [(i, i ^ bit) for i in range(lax.axis_size('z'))])  3.97 us
  transfers between devices with their start and end apart: 8, of which 6 were waited for; matrix products, arithmetic and copies ran while one was open for 0% of the time, Pallas kernels for 0%

profile of v6, /device:TPU:1, one launch (start us, length us, event | category | flops | bytes accessed | tf_op | source)
XLA Modules:
  0.0 98.9 jit_solution(4609237919854450991)
XLA Ops:
  0.6 0.7 slice_bitcast_fusion
  1.4 1.3 %collective-permute-start.1 = (bf16[2,512]{1,0:T(2,128)(2,1)S(1)}, bf16[2,512]{1,0:T(2,128)(2,1)S(1)}, u32[]{:S(2)}, u32[]{:S(2)}) collective-permute-start(bf16[2,512]{1,0:T(2,128)(2,1)S(1)} %get-tuple-element.8), channel_id=1, source_target_pairs={{8,0},{16,8},{24,16},{32,24},{40,32},{48,40},{56,48},{64,56},{72,6... | collective-permute-start | bytes 6152 | tf_op jit(solution)/shard_map/ppermute | solution.py:28
  2.6 5.0 %collective-permute-start = (bf16[2,512]{1,0:T(2,128)(2,1)S(1)}, bf16[2,512]{1,0:T(2,128)(2,1)S(1)}, u32[]{:S(2)}, u32[]{:S(2)}) collective-permute-start(bf16[2,512]{1,0:T(2,128)(2,1)S(1)} %get-tuple-element.9), channel_id=1, source_target_pairs={{0,8},{8,16},{16,24},{24,32},{32,40},{40,48},{48,56},{56,64},{64,7... | collective-permute-start | bytes 6152 | tf_op jit(solution)/shard_map/ppermute | solution.py:27
  7.7 0.0 collective-permute-done.1.behind_hbm
  7.7 0.7 collective-permute-done.ahead_hbm
  8.4 7.3 %front.1 = (bf16[1024,512]{1,0:T(8,128)(2,1)}, f32[1664,128]{1,0:T(8,128)S(1)}, f32[1664,128]{1,0:T(8,128)S(1)}) custom-call(s32[1]{0:T(128)} %bitcast.core_ref, bf16[1024,512]{1,0:T(8,128)(2,1)} %bitcast.18, bf16[2,512]{1,0:T(2,128)(2,1)S(1)} %collective-permute-done.ahead_hbm, bf16[2,512]{1,0:T(2,128)(2,1)S(1)} %collective-permute-done.1.behind_hbm, ...), custom_call_target="tpu_custom_call" | custom-call | tf_op jit(solution)/shard_map/front/pallas_call | solution.py:181
  15.7 3.5 %collective-permute-start.2 = (f32[1664,128]{1,0:T(8,128)S(1)}, f32[1664,128]{1,0:T(8,128)S(1)}, u32[]{:S(2)}, u32[]{:S(2)}) collective-permute-start(f32[1664,128]{1,0:T(8,128)S(1)} %get-tuple-element.7), channel_id=1, source_target_pairs={{0,1},{1,0},{2,3},{3,2},{4,5},{5,4},{6,7},{7,6},{8,9},{9,8},{10,11... | collective-permute-start | bytes 2555912 | tf_op jit(solution)/shard_map/ppermute | solution.py:34
  19.2 2.0 %collective-permute-done.2 = f32[1664,128]{1,0:T(8,128)S(1)} collective-permute-done((f32[1664,128]{1,0:T(8,128)S(1)}, f32[1664,128]{1,0:T(8,128)S(1)}, u32[]{:S(2)}, u32[]{:S(2)}) %collective-permute-start.2) | collective-permute-done | bytes 852000 | tf_op jit(solution)/shard_map/ppermute | solution.py:34
  21.2 0.1 add.15
  21.3 26.7 %all_to_all.10 = f32[16,104,128]{2,1,0:T(8,128)S(1)} all-to-all(f32[16,104,128]{2,1,0:T(8,128)S(1)} %bitcast.15), channel_id=1, replica_groups=mesh['x'=4,'z'=8,'y'=4,'core'=2] {'x','y'}, dimensions={0} | all-to-all | bytes 1703936 | tf_op jit(solution)/shard_map/all_to_all | solution.py:37
  48.1 0.3 collective-permute-start.3
  48.4 6.6 %collective-permute-done.3 = f32[104,128]{1,0:T(8,128)S(1)} collective-permute-done((f32[104,128]{1,0:T(8,128)S(1)}, f32[104,128]{1,0:T(8,128)S(1)}, u32[]{:S(2)}, u32[]{:S(2)}) %collective-permute-start.3) | collective-permute-done | bytes 53280 | tf_op jit(solution)/shard_map/ppermute | solution.py:43
  55.1 0.1 collective-permute-start.6
  55.2 0.1 collective-permute-start.5
  55.3 3.4 %collective-permute-start.4 = (f32[104,128]{1,0:T(8,128)S(1)}, f32[104,128]{1,0:T(8,128)S(1)}, u32[]{:S(2)}, u32[]{:S(2)}) collective-permute-start(f32[104,128]{1,0:T(8,128)S(1)} %add.16), channel_id=1, source_target_pairs={{0,8},{8,0},{16,24},{24,16},{32,40},{40,32},{48,56},{56,48},{1,9},... | collective-permute-start | bytes 159752 | tf_op jit(solution)/shard_map/ppermute | solution.py:43
  58.7 1.4 %collective-permute-done.6 = f32[104,128]{1,0:T(8,128)S(1)} collective-permute-done((f32[104,128]{1,0:T(8,128)S(1)}, f32[104,128]{1,0:T(8,128)S(1)}, u32[]{:S(2)}, u32[]{:S(2)}) %collective-permute-start.6) | collective-permute-done | bytes 53280 | tf_op jit(solution)/shard_map/ppermute | solution.py:43
  60.1 0.0 collective-permute-done.5
  60.1 0.5 collective-permute-done.4
  60.6 0.1 broadcast_in_dim.19
  60.7 14.3 %all_to_all.11 = f32[16,104,128]{2,1,0:T(8,128)S(1)} all-to-all(f32[16,104,128]{2,1,0:T(8,128)S(1)} %broadcast_in_dim.19), channel_id=1, replica_groups=mesh['x'=4,'z'=8,'y'=4,'core'=2] {'x','y'}, dimensions={0} | all-to-all | bytes 1703936 | tf_op jit(solution)/shard_map/all_to_all | solution.py:47
  75.0 5.2 %collective-permute-start.7 = (f32[1664,128]{1,0:T(8,128)S(1)}, f32[1664,128]{1,0:T(8,128)S(1)}, u32[]{:S(2)}, u32[]{:S(2)}) collective-permute-start(f32[1664,128]{1,0:T(8,128)S(1)} %bitcast.13), channel_id=1, source_target_pairs={{0,1},{1,0},{2,3},{3,2},{4,5},{5,4},{6,7},{7,6},{8,9},{9,8},{10,11... | collective-permute-start | bytes 2555912 | tf_op jit(solution)/shard_map/ppermute | solution.py:49
  80.2 2.0 %collective-permute-done.7.other_ref = f32[1664,128]{1,0:T(8,128)S(1)} collective-permute-done((f32[1664,128]{1,0:T(8,128)S(1)}, f32[1664,128]{1,0:T(8,128)S(1)}, u32[]{:S(2)}, u32[]{:S(2)}) %collective-permute-start.7) | collective-permute-done | bytes 852000 | tf_op jit(solution)/shard_map/ppermute | solution.py:49
  82.2 16.5 %ridge_solve.1 = f32[512,512]{1,0:T(8,128)} custom-call(s32[1]{0:T(128)} %bitcast.core_ref, f32[1664,128]{1,0:T(8,128)S(1)} %bitcast.14, f32[1664,128]{1,0:T(8,128)S(1)} %collective-permute-done.7.other_ref), custom_call_target="tpu_custom_call" | custom-call | tf_op jit(solution)/shard_map/ridge_solve/pallas_call | solution.py:402
  (3 shorter events, 0.1 us)
Async XLA Ops:
  1.4 6.3 %collective-permute-start.1 = (bf16[2,512]{1,0:T(2,128)(2,1)S(1)}, bf16[2,512]{1,0:T(2,128)(2,1)S(1)}, u32[]{:S(2)}, u32[]{:S(2)}) collective-permute-start(bf16[2,512]{1,0:T(2,128)(2,1)S(1)} %get-tuple-element.8), channel_id=1, source_target_pairs={{8,0},{16,8},{24,16},{32,24},{40,32},{48,40},{56,48},{64,56},{72,6... | collective-permute-start | bytes 6152 | tf_op jit(solution)/shard_map/ppermute | solution.py:28
  2.6 5.7 %collective-permute-start = (bf16[2,512]{1,0:T(2,128)(2,1)S(1)}, bf16[2,512]{1,0:T(2,128)(2,1)S(1)}, u32[]{:S(2)}, u32[]{:S(2)}) collective-permute-start(bf16[2,512]{1,0:T(2,128)(2,1)S(1)} %get-tuple-element.9), channel_id=1, source_target_pairs={{0,8},{8,16},{16,24},{24,32},{32,40},{40,48},{48,56},{56,64},{64,7... | collective-permute-start | bytes 6152 | tf_op jit(solution)/shard_map/ppermute | solution.py:27
  15.7 5.5 %collective-permute-start.2 = (f32[1664,128]{1,0:T(8,128)S(1)}, f32[1664,128]{1,0:T(8,128)S(1)}, u32[]{:S(2)}, u32[]{:S(2)}) collective-permute-start(f32[1664,128]{1,0:T(8,128)S(1)} %get-tuple-element.7), channel_id=1, source_target_pairs={{0,1},{1,0},{2,3},{3,2},{4,5},{5,4},{6,7},{7,6},{8,9},{9,8},{10,11... | collective-permute-start | bytes 2555912 | tf_op jit(solution)/shard_map/ppermute | solution.py:34
  48.1 7.0 %collective-permute-start.3 = (f32[104,128]{1,0:T(8,128)S(1)}, f32[104,128]{1,0:T(8,128)S(1)}, u32[]{:S(2)}, u32[]{:S(2)}) collective-permute-start(f32[104,128]{1,0:T(8,128)S(1)} %reduce_sum.9), channel_id=1, source_target_pairs={{0,32},{8,40},{16,48},{24,56},{32,0},{40,8},{48,16},{56,24},{1,33}... | collective-permute-start | bytes 159752 | tf_op jit(solution)/shard_map/ppermute | solution.py:43
  55.1 5.0 %collective-permute-start.6 = (f32[104,128]{1,0:T(8,128)S(1)}, f32[104,128]{1,0:T(8,128)S(1)}, u32[]{:S(2)}, u32[]{:S(2)}) collective-permute-start(f32[104,128]{1,0:T(8,128)S(1)} %add.16), channel_id=1, source_target_pairs={{0,24},{8,16},{16,8},{24,0},{32,56},{40,48},{48,40},{56,32},{1,25}... | collective-permute-start | bytes 159752 | tf_op jit(solution)/shard_map/ppermute | solution.py:43
  55.2 4.9 %collective-permute-start.5 = (f32[104,128]{1,0:T(8,128)S(1)}, f32[104,128]{1,0:T(8,128)S(1)}, u32[]{:S(2)}, u32[]{:S(2)}) collective-permute-start(f32[104,128]{1,0:T(8,128)S(1)} %add.16), channel_id=1, source_target_pairs={{0,16},{8,24},{16,0},{24,8},{32,48},{40,56},{48,32},{56,40},{1,17}... | collective-permute-start | bytes 159752 | tf_op jit(solution)/shard_map/ppermute | solution.py:43
  55.3 5.3 %collective-permute-start.4 = (f32[104,128]{1,0:T(8,128)S(1)}, f32[104,128]{1,0:T(8,128)S(1)}, u32[]{:S(2)}, u32[]{:S(2)}) collective-permute-start(f32[104,128]{1,0:T(8,128)S(1)} %add.16), channel_id=1, source_target_pairs={{0,8},{8,0},{16,24},{24,16},{32,40},{40,32},{48,56},{56,48},{1,9},... | collective-permute-start | bytes 159752 | tf_op jit(solution)/shard_map/ppermute | solution.py:43
  75.0 7.2 %collective-permute-start.7 = (f32[1664,128]{1,0:T(8,128)S(1)}, f32[1664,128]{1,0:T(8,128)S(1)}, u32[]{:S(2)}, u32[]{:S(2)}) collective-permute-start(f32[1664,128]{1,0:T(8,128)S(1)} %bitcast.13), channel_id=1, source_target_pairs={{0,1},{1,0},{2,3},{3,2},{4,5},{5,4},{6,7},{7,6},{8,9},{9,8},{10,11... | collective-permute-start | bytes 2555912 | tf_op jit(solution)/shard_map/ppermute | solution.py:49

commit v7 on v6

--- a/solution.py
+++ b/solution.py
@@ -158,11 +158,14 @@
                 block = jnp.concatenate([block[:middle], riding, block[middle + 8 :]], axis=0)
             owner, place = divmod(n, half)
             halves[owner, place * BLOCK : (place + 1) * BLOCK, :] = block
-    for side, target in ((core, keep_hbm), (1 - core, send_hbm)):
-        stores.append(
+        side = first // 2
+        leave = [
             pltpu.make_async_copy(halves.at[side], target, sems.at[len(loads) + len(stores)])
-        )
-        stores[-1].start()
+            for target in (keep_hbm, send_hbm)
+        ]
+        pl.when(core == side)(leave[0].start)
+        pl.when(core != side)(leave[1].start)
+        stores.append(leave[0])
     for store in stores:
         store.wait()
 

time: 99.3 us -> 99.6 us (level)
  no operation moved by 1% of the time
where the time goes in v7:
time: 99.6 us; the launch traced here: 99.2 us
  blocking collectives  41 us (41%)
  Pallas kernels  24.2 us (24%)
  starting transfers between devices  18.9 us (19%)
  waiting for transfers between devices  13.3 us (13%)
    all_to_all x1, blocking collectives, all_sum(): lax.all_to_all(part.reshape(peers, rows, BLOCK), ('x', 'y'), split_axis=0...  26.7 us
    pallas_call x1, Pallas kernels, ridge_solve(): pl.pallas_call(functools.partial(solve_kernel, kept, row_blocks, col_bloc...  16.5 us
    all_to_all x1, blocking collectives, all_sum(): lax.all_to_all(spread, ('x', 'y'), split_axis=0, concat_axis=0, tiled=True)  14.3 us
    ppermute x4, waiting for transfers between devices, all_sum(): lax.ppermute(chunk, 'z', [(i, i ^ bit) for i in range(lax.axis_size('z'))])  8.54 us
    pallas_call x1, Pallas kernels, front(): pl.pallas_call(functools.partial(front_kernel, kept), out_shape=[jax.Shap...  7.63 us
    ppermute x1, starting transfers between devices, all_sum(): other = lax.ppermute(mine, 'core', swap)  5.17 us
    ppermute x1, starting transfers between devices, frame_halo(): before = lax.ppermute(rows[-width:], ('x', 'z'), up)  5 us
    ppermute x4, starting transfers between devices, all_sum(): lax.ppermute(chunk, 'z', [(i, i ^ bit) for i in range(lax.axis_size('z'))])  3.97 us
  transfers between devices with their start and end apart: 8, of which 6 were waited for; matrix products, arithmetic and copies ran while one was open for 0% of the time, Pallas kernels for 0%

profile of v7, /device:TPU:1, one launch (start us, length us, event | category | flops | bytes accessed | tf_op | source)
XLA Modules:
  0.0 99.2 jit_solution(11019459482766246179)
XLA Ops:
  0.6 0.7 slice_bitcast_fusion
  1.4 1.3 %collective-permute-start.1 = (bf16[2,512]{1,0:T(2,128)(2,1)S(1)}, bf16[2,512]{1,0:T(2,128)(2,1)S(1)}, u32[]{:S(2)}, u32[]{:S(2)}) collective-permute-start(bf16[2,512]{1,0:T(2,128)(2,1)S(1)} %get-tuple-element.8), channel_id=1, source_target_pairs={{8,0},{16,8},{24,16},{32,24},{40,32},{48,40},{56,48},{64,56},{72,6... | collective-permute-start | bytes 6152 | tf_op jit(solution)/shard_map/ppermute | solution.py:28
  2.6 5.0 %collective-permute-start = (bf16[2,512]{1,0:T(2,128)(2,1)S(1)}, bf16[2,512]{1,0:T(2,128)(2,1)S(1)}, u32[]{:S(2)}, u32[]{:S(2)}) collective-permute-start(bf16[2,512]{1,0:T(2,128)(2,1)S(1)} %get-tuple-element.9), channel_id=1, source_target_pairs={{0,8},{8,16},{16,24},{24,32},{32,40},{40,48},{48,56},{56,64},{64,7... | collective-permute-start | bytes 6152 | tf_op jit(solution)/shard_map/ppermute | solution.py:27
  7.7 0.0 collective-permute-done.1.behind_hbm
  7.7 0.7 collective-permute-done.ahead_hbm
  8.4 7.6 %front.1 = (bf16[1024,512]{1,0:T(8,128)(2,1)}, f32[1664,128]{1,0:T(8,128)S(1)}, f32[1664,128]{1,0:T(8,128)S(1)}) custom-call(s32[1]{0:T(128)} %bitcast.core_ref, bf16[1024,512]{1,0:T(8,128)(2,1)} %bitcast.18, bf16[2,512]{1,0:T(2,128)(2,1)S(1)} %collective-permute-done.ahead_hbm, bf16[2,512]{1,0:T(2,128)(2,1)S(1)} %collective-permute-done.1.behind_hbm, ...), custom_call_target="tpu_custom_call" | custom-call | tf_op jit(solution)/shard_map/front/pallas_call | solution.py:184
  16.0 3.5 %collective-permute-start.2 = (f32[1664,128]{1,0:T(8,128)S(1)}, f32[1664,128]{1,0:T(8,128)S(1)}, u32[]{:S(2)}, u32[]{:S(2)}) collective-permute-start(f32[1664,128]{1,0:T(8,128)S(1)} %get-tuple-element.7), channel_id=1, source_target_pairs={{0,1},{1,0},{2,3},{3,2},{4,5},{5,4},{6,7},{7,6},{8,9},{9,8},{10,11... | collective-permute-start | bytes 2555912 | tf_op jit(solution)/shard_map/ppermute | solution.py:34
  19.5 2.0 %collective-permute-done.2 = f32[1664,128]{1,0:T(8,128)S(1)} collective-permute-done((f32[1664,128]{1,0:T(8,128)S(1)}, f32[1664,128]{1,0:T(8,128)S(1)}, u32[]{:S(2)}, u32[]{:S(2)}) %collective-permute-start.2) | collective-permute-done | bytes 852000 | tf_op jit(solution)/shard_map/ppermute | solution.py:34
  21.5 0.1 add.15
  21.6 26.7 %all_to_all.10 = f32[16,104,128]{2,1,0:T(8,128)S(1)} all-to-all(f32[16,104,128]{2,1,0:T(8,128)S(1)} %bitcast.15), channel_id=1, replica_groups=mesh['x'=4,'z'=8,'y'=4,'core'=2] {'x','y'}, dimensions={0} | all-to-all | bytes 1703936 | tf_op jit(solution)/shard_map/all_to_all | solution.py:37
  48.4 0.3 collective-permute-start.3
  48.7 6.6 %collective-permute-done.3 = f32[104,128]{1,0:T(8,128)S(1)} collective-permute-done((f32[104,128]{1,0:T(8,128)S(1)}, f32[104,128]{1,0:T(8,128)S(1)}, u32[]{:S(2)}, u32[]{:S(2)}) %collective-permute-start.3) | collective-permute-done | bytes 53280 | tf_op jit(solution)/shard_map/ppermute | solution.py:43
  55.4 0.1 collective-permute-start.6
  55.5 0.1 collective-permute-start.5
  55.6 3.4 %collective-permute-start.4 = (f32[104,128]{1,0:T(8,128)S(1)}, f32[104,128]{1,0:T(8,128)S(1)}, u32[]{:S(2)}, u32[]{:S(2)}) collective-permute-start(f32[104,128]{1,0:T(8,128)S(1)} %add.16), channel_id=1, source_target_pairs={{0,8},{8,0},{16,24},{24,16},{32,40},{40,32},{48,56},{56,48},{1,9},... | collective-permute-start | bytes 159752 | tf_op jit(solution)/shard_map/ppermute | solution.py:43
  59.0 1.4 %collective-permute-done.6 = f32[104,128]{1,0:T(8,128)S(1)} collective-permute-done((f32[104,128]{1,0:T(8,128)S(1)}, f32[104,128]{1,0:T(8,128)S(1)}, u32[]{:S(2)}, u32[]{:S(2)}) %collective-permute-start.6) | collective-permute-done | bytes 53280 | tf_op jit(solution)/shard_map/ppermute | solution.py:43
  60.4 0.0 collective-permute-done.5
  60.4 0.5 collective-permute-done.4
  60.9 0.1 broadcast_in_dim.19
  61.0 14.3 %all_to_all.11 = f32[16,104,128]{2,1,0:T(8,128)S(1)} all-to-all(f32[16,104,128]{2,1,0:T(8,128)S(1)} %broadcast_in_dim.19), channel_id=1, replica_groups=mesh['x'=4,'z'=8,'y'=4,'core'=2] {'x','y'}, dimensions={0} | all-to-all | bytes 1703936 | tf_op jit(solution)/shard_map/all_to_all | solution.py:47
  75.3 5.2 %collective-permute-start.7 = (f32[1664,128]{1,0:T(8,128)S(1)}, f32[1664,128]{1,0:T(8,128)S(1)}, u32[]{:S(2)}, u32[]{:S(2)}) collective-permute-start(f32[1664,128]{1,0:T(8,128)S(1)} %bitcast.13), channel_id=1, source_target_pairs={{0,1},{1,0},{2,3},{3,2},{4,5},{5,4},{6,7},{7,6},{8,9},{9,8},{10,11... | collective-permute-start | bytes 2555912 | tf_op jit(solution)/shard_map/ppermute | solution.py:49
  80.5 2.0 %collective-permute-done.7.other_ref = f32[1664,128]{1,0:T(8,128)S(1)} collective-permute-done((f32[1664,128]{1,0:T(8,128)S(1)}, f32[1664,128]{1,0:T(8,128)S(1)}, u32[]{:S(2)}, u32[]{:S(2)}) %collective-permute-start.7) | collective-permute-done | bytes 852000 | tf_op jit(solution)/shard_map/ppermute | solution.py:49
  82.5 16.5 %ridge_solve.1 = f32[512,512]{1,0:T(8,128)} custom-call(s32[1]{0:T(128)} %bitcast.core_ref, f32[1664,128]{1,0:T(8,128)S(1)} %bitcast.14, f32[1664,128]{1,0:T(8,128)S(1)} %collective-permute-done.7.other_ref), custom_call_target="tpu_custom_call" | custom-call | tf_op jit(solution)/shard_map/ridge_solve/pallas_call | solution.py:405
  (3 shorter events, 0.1 us)
Async XLA Ops:
  1.4 6.3 %collective-permute-start.1 = (bf16[2,512]{1,0:T(2,128)(2,1)S(1)}, bf16[2,512]{1,0:T(2,128)(2,1)S(1)}, u32[]{:S(2)}, u32[]{:S(2)}) collective-permute-start(bf16[2,512]{1,0:T(2,128)(2,1)S(1)} %get-tuple-element.8), channel_id=1, source_target_pairs={{8,0},{16,8},{24,16},{32,24},{40,32},{48,40},{56,48},{64,56},{72,6... | collective-permute-start | bytes 6152 | tf_op jit(solution)/shard_map/ppermute | solution.py:28
  2.6 5.7 %collective-permute-start = (bf16[2,512]{1,0:T(2,128)(2,1)S(1)}, bf16[2,512]{1,0:T(2,128)(2,1)S(1)}, u32[]{:S(2)}, u32[]{:S(2)}) collective-permute-start(bf16[2,512]{1,0:T(2,128)(2,1)S(1)} %get-tuple-element.9), channel_id=1, source_target_pairs={{0,8},{8,16},{16,24},{24,32},{32,40},{40,48},{48,56},{56,64},{64,7... | collective-permute-start | bytes 6152 | tf_op jit(solution)/shard_map/ppermute | solution.py:27
  16.0 5.5 %collective-permute-start.2 = (f32[1664,128]{1,0:T(8,128)S(1)}, f32[1664,128]{1,0:T(8,128)S(1)}, u32[]{:S(2)}, u32[]{:S(2)}) collective-permute-start(f32[1664,128]{1,0:T(8,128)S(1)} %get-tuple-element.7), channel_id=1, source_target_pairs={{0,1},{1,0},{2,3},{3,2},{4,5},{5,4},{6,7},{7,6},{8,9},{9,8},{10,11... | collective-permute-start | bytes 2555912 | tf_op jit(solution)/shard_map/ppermute | solution.py:34
  48.4 7.0 %collective-permute-start.3 = (f32[104,128]{1,0:T(8,128)S(1)}, f32[104,128]{1,0:T(8,128)S(1)}, u32[]{:S(2)}, u32[]{:S(2)}) collective-permute-start(f32[104,128]{1,0:T(8,128)S(1)} %reduce_sum.9), channel_id=1, source_target_pairs={{0,32},{8,40},{16,48},{24,56},{32,0},{40,8},{48,16},{56,24},{1,33}... | collective-permute-start | bytes 159752 | tf_op jit(solution)/shard_map/ppermute | solution.py:43
  55.4 5.0 %collective-permute-start.6 = (f32[104,128]{1,0:T(8,128)S(1)}, f32[104,128]{1,0:T(8,128)S(1)}, u32[]{:S(2)}, u32[]{:S(2)}) collective-permute-start(f32[104,128]{1,0:T(8,128)S(1)} %add.16), channel_id=1, source_target_pairs={{0,24},{8,16},{16,8},{24,0},{32,56},{40,48},{48,40},{56,32},{1,25}... | collective-permute-start | bytes 159752 | tf_op jit(solution)/shard_map/ppermute | solution.py:43
  55.5 4.9 %collective-permute-start.5 = (f32[104,128]{1,0:T(8,128)S(1)}, f32[104,128]{1,0:T(8,128)S(1)}, u32[]{:S(2)}, u32[]{:S(2)}) collective-permute-start(f32[104,128]{1,0:T(8,128)S(1)} %add.16), channel_id=1, source_target_pairs={{0,16},{8,24},{16,0},{24,8},{32,48},{40,56},{48,32},{56,40},{1,17}... | collective-permute-start | bytes 159752 | tf_op jit(solution)/shard_map/ppermute | solution.py:43
  55.6 5.3 %collective-permute-start.4 = (f32[104,128]{1,0:T(8,128)S(1)}, f32[104,128]{1,0:T(8,128)S(1)}, u32[]{:S(2)}, u32[]{:S(2)}) collective-permute-start(f32[104,128]{1,0:T(8,128)S(1)} %add.16), channel_id=1, source_target_pairs={{0,8},{8,0},{16,24},{24,16},{32,40},{40,32},{48,56},{56,48},{1,9},... | collective-permute-start | bytes 159752 | tf_op jit(solution)/shard_map/ppermute | solution.py:43
  75.3 7.2 %collective-permute-start.7 = (f32[1664,128]{1,0:T(8,128)S(1)}, f32[1664,128]{1,0:T(8,128)S(1)}, u32[]{:S(2)}, u32[]{:S(2)}) collective-permute-start(f32[1664,128]{1,0:T(8,128)S(1)} %bitcast.13), channel_id=1, source_target_pairs={{0,1},{1,0},{2,3},{3,2},{4,5},{5,4},{6,7},{7,6},{8,9},{9,8},{10,11... | collective-permute-start | bytes 2555912 | tf_op jit(solution)/shard_map/ppermute | solution.py:49
